TPU v7x, 32 devices: a whole 2x2x4 slice. The times are simulated.
32 devices in a mesh: ctx: 8 (over z, y), tp: 2 (over x), dp: 2 (over core).
Axes of the slice: x: 2, y: 2, z: 4, core: 2. Of those that a mesh axis runs over, the one named last changes fastest.
Arguments:
- vis_qkv: bfloat16 [8192, 3, 1280], P(('dp', 'ctx'), None, 'tp'), parts along dimension 0, may hold values from -60 to 60
- vis_resid: bfloat16 [8192, 1280], P(('dp', 'ctx'), 'tp'), parts along dimension 0, may hold values from -1.796875 to 1.796875
- vis_out_w: bfloat16 [1280, 1280], P(None, 'tp'), may hold values from -0.15625 to 0.15625
- merge_gain: float32 [1280], P('tp'), may hold values from 0.5 to 1.5
- merge_bias: float32 [1280], P('tp'), may hold values from -3 to 3
- vis_kv_w: bfloat16 [4, 1280, 2048], P(None, 'tp'), may hold values from -0.078125 to 0.078125
- frame_host: int32 [16], P('dp'), parts along dimension 0, may hold values from 0 to 7, as said below
- vis_pos: int32 [16], P('dp'), parts along dimension 0, may hold values from 0 to 1920, as said below
- doc_ids: int32 [4096], P('dp'), parts along dimension 0, may hold values from 0 to 3, as said below
- text_kv: bfloat16 [4096, 8, 2, 128], P(('dp', 'ctx'), 'tp'), parts along dimension 0, may hold values from -4 to 4
- queries: bfloat16 [4096, 4096], P(('dp', 'ctx'), 'tp'), parts along dimension 0, may hold values from -50 to 50
Outputs:
- attended: bfloat16 [4096, 4096], P(('dp', 'ctx'), 'tp'), parts along dimension 0
There are 2 independent parts, one for each index of `dp`. A program takes and returns all parts, laid end to end along the dimension named above; an argument that names none is the same for every part. Nothing has to cross between parts.
Inputs may be any that keep to these rules, and one draw needn't show every extreme that they name: `vis_pos`: frame starts are multiples of 128 and increase with the frame; some block of 256 positions holds only frames. `frame_host`: each frame is encoded on the ctx device that holds its positions or on the device 8 / 2 indices away along ctx; every device encodes exactly 1 frame. `doc_ids`: never falls along the sequence.
All inputs are finite; a program needn't handle non-finite values.
Results may differ from a plain program's by a relative error of at most 0.0085.
Values may be sent and summed in bfloat16 or wider, within the bound.
No kernel may reach another device: no remote copies, remote signals or barrier semaphores. Data moves between devices by JAX's collectives and lax.ppermute only.
A program may use at most 64 MiB of HBM per device.

v0:
```python
import functools
import math

import jax
import jax.numpy as jnp
from jax import lax
from jax.experimental import pallas as pl
from jax.experimental.pallas import tpu as pltpu
from jax.sharding import PartitionSpec as P

VD = 1280
VH = 16
HD = 128
H = 32
KVH = 8
FT = 128
GROUP = H // KVH
DOCS = 4
LANES = 128

MASKED = -1e30
VMEM_LIMIT = 16 * 1024 * 1024
MERGE_VMEM = 52 * 1024 * 1024
LANGUAGE_VMEM = 58 * 1024 * 1024


def contract_last(a, b):
    return lax.dot_general(a, b, (((1,), (1,)), ((), ())), preferred_element_type=jnp.float32)


def shifted(block, axis, distance):
    count = lax.axis_size(axis)
    return lax.ppermute(block, axis, [(i, (i + distance) % count) for i in range(count)])


def ring_place(row, rows):
    return jnp.where(row % 2 == 1, (row + 1) // 2, (rows - row // 2) % rows)


def to_next_row(block, rows):
    order = [0] + list(range(1, rows, 2)) + list(range(rows - 2, 0, -2))
    after = dict(zip(order, order[1:] + order[:1]))
    return lax.ppermute(
        block,
        "ctx",
        [(2 * row + side, 2 * after[row] + side) for row in range(rows) for side in range(2)],
    )


def to_other_side(block, rows):
    return lax.ppermute(
        block, "ctx", [(2 * row + side, 2 * row + 1 - side) for row in range(rows) for side in range(2)]
    )


class Ring:
    def __init__(self, block, rows):
        self.rows = rows
        self.blocks = [block]
        self.start(block)

    def start(self, block):
        self.moving = to_next_row(block, self.rows) if len(self.blocks) < 2 * self.rows - 1 else None
        self.blocks.append(to_other_side(block, self.rows))

    def advance(self, beside, lag=0):
        if self.moving is None:
            return beside
        if len(self.blocks) > 2 * lag:
            at = len(self.blocks) - 1 - 2 * lag
            held, self.blocks[at], beside = lax.optimization_barrier(
                (self.moving, self.blocks[at], beside)
            )
        else:
            held, beside = lax.optimization_barrier((self.moving, beside))
        self.blocks.append(held)
        self.start(held)
        return beside

    def all(self):
        while self.moving is not None:
            self.advance(())
        return self.blocks


def vit_kernel(index_ref, q_ref, k_ref, v_ref, after_ref, *rest, heads, dim):
    o_ref = rest[0]
    if len(rest) > 1:
        earlier_ref, weight_ref, resid_ref, o_ref, low_ref, high_ref = rest
    width = q_ref.shape[2]
    to_exp = 1.0 / math.sqrt(dim)
    tiles = {}
    for g in range(heads):
        first, last = g * dim, (g + 1) * dim
        low = first // LANES * LANES
        high = min(width, -(-last // LANES) * LANES)
        lane = lax.broadcasted_iota(jnp.int32, (1, high - low), 1) + low
        inside = (lane >= first) & (lane < last)
        keep = jnp.where(inside, 1.0, 0.0).astype(jnp.bfloat16)
        other = jnp.where(inside, 0.0, 1.0).astype(jnp.bfloat16)
        scores = contract_last(q_ref[0, :, low:high] * keep, k_ref[0, :, low:high])
        row_max = jnp.max(scores, axis=1, keepdims=True)
        weights = jnp.exp((scores - row_max) * to_exp).astype(jnp.bfloat16)
        mixed = jnp.dot(
            weights, v_ref[0, :, low:high] * keep + other, preferred_element_type=jnp.float32
        )
        spare = 0 if low < first else last - low
        mixed = mixed / mixed[:, spare : spare + 1]
        for at in range(low, high, LANES):
            end = min(at + LANES, high)
            piece = mixed[:, at - low : end - low]
            if at in tiles:
                piece = jnp.where(inside[:, at - low : end - low], piece, tiles[at])
            tiles[at] = piece
    for at, piece in tiles.items():
        o_ref[:, at : at + piece.shape[1]] = piece.astype(o_ref.dtype)
    if len(rest) > 1:
        rows = o_ref.shape[0]
        for part, (context, hidden_ref) in enumerate([(earlier_ref, low_ref), (o_ref, high_ref)]):
            here = slice(part * rows, (part + 1) * rows)
            hidden_ref[...] = resid_ref[here].astype(jnp.float32) + jnp.dot(
                context[...], weight_ref[...], preferred_element_type=jnp.float32
            )


def vit_attention(fields, after, part, tp_index, projection=None):
    _, patches, width = fields.shape
    rows = patches // 2
    dim = VD // VH
    one = pl.BlockSpec((rows, width), lambda f, _: (0, 0))
    in_specs = [
        pl.BlockSpec((1, rows, width), lambda f, _: (0, part, 0)),
        pl.BlockSpec((1, patches, width), lambda f, _: (1, 0, 0)),
        pl.BlockSpec((1, patches, width), lambda f, _: (2, 0, 0)),
        pl.BlockSpec(memory_space=pl.ANY),
    ]
    out_specs = [one]
    out_shape = [jax.ShapeDtypeStruct((rows, width), jnp.bfloat16)]
    if projection:
        in_specs += [
            one,
            pl.BlockSpec((width, width), lambda f, index: (index[0], 0)),
            pl.BlockSpec((patches, width), lambda f, _: (0, 0)),
        ]
        out_specs += [one, one]
        out_shape += [jax.ShapeDtypeStruct((rows, width), jnp.float32)] * 2
    return pl.pallas_call(
        functools.partial(vit_kernel, heads=width // dim, dim=dim),
        grid_spec=pltpu.PrefetchScalarGridSpec(
            num_scalar_prefetch=1, grid=(1,), in_specs=in_specs, out_specs=out_specs
        ),
        out_shape=out_shape,
        compiler_params=pltpu.CompilerParams(
            vmem_limit_bytes=VMEM_LIMIT
        ),
        cost_estimate=pl.CostEstimate(flops=1024, bytes_accessed=1024, transcendentals=0),
    )(jnp.reshape(tp_index, (1,)), fields, fields, fields, after, *(projection or ()))


def merge_kernel(block_ref, x_ref, w_ref, o_ref, held_ref, rows_ref, sems):
    tokens, columns = o_ref.shape
    patches = x_ref.shape[0]

    def weights_in(j):
        lanes = pl.ds(pl.multiple_of(block_ref[0] * columns, columns), columns)
        return pltpu.make_async_copy(w_ref.at[j, :, lanes], held_ref.at[j], sems.at[j])

    for j in range(4):
        weights_in(j).start()
    token = lax.broadcasted_iota(jnp.int32, (tokens, patches), 0)
    patch = lax.broadcasted_iota(jnp.int32, (tokens, patches), 1)
    for j in range(4):
        pick = jnp.where(patch == 4 * token + j, 1.0, 0.0).astype(jnp.bfloat16)
        rows_ref[j] = jnp.dot(pick, x_ref[...], preferred_element_type=jnp.float32).astype(
            jnp.bfloat16
        )
    total = None
    for j in range(4):
        weights_in(j).wait()
        product = jnp.dot(rows_ref[j], held_ref[j], preferred_element_type=jnp.float32)
        total = product if total is None else total + product
    o_ref[...] = total.astype(o_ref.dtype)


def merged_columns(normed, weights, block, columns, dtype):
    patches, width = normed.shape
    tokens = patches // 4
    return pl.pallas_call(
        merge_kernel,
        in_specs=[
            pl.BlockSpec(memory_space=pltpu.SMEM),
            pl.BlockSpec(memory_space=pltpu.VMEM),
            pl.BlockSpec(memory_space=pl.ANY),
        ],
        out_specs=pl.BlockSpec(memory_space=pltpu.VMEM),
        out_shape=jax.ShapeDtypeStruct((tokens, columns), dtype),
        scratch_shapes=[
            pltpu.VMEM((4, width, columns), jnp.bfloat16),
            pltpu.VMEM((4, tokens, width), jnp.bfloat16),
            pltpu.SemaphoreType.DMA((4,)),
        ],
        compiler_params=pltpu.CompilerParams(vmem_limit_bytes=MERGE_VMEM),
        cost_estimate=pl.CostEstimate(
            flops=2 * tokens * 4 * width * columns,
            bytes_accessed=4 * width * columns * 2 + patches * width * 2,
            transcendentals=0,
        ),
    )(jnp.reshape(block, (1,)), normed, weights)


def tables_kernel(
    device_ref, vis_pos_ref, frame_host_ref, doc_ref, place_ref, *, peers, per_device,
):
    device = device_ref[0]
    rows = peers // 2
    frames = vis_pos_ref.shape[0]
    slots_each = per_device // FT
    first_pos = device * per_device
    starts = [
        jnp.sum(jnp.where(doc_ref[...] < d, 1.0, 0.0)).astype(jnp.int32) for d in range(1, DOCS)
    ]
    for i, value in enumerate([first_pos] + starts):
        place_ref[2 * peers + i] = value

    def block_from(source):
        hop = lax.rem(ring_place(device // 2, rows) + rows - ring_place(source // 2, rows), rows)
        return 2 * hop + jnp.where(lax.rem(source, 2) == lax.rem(device, 2), 0, 1)

    def one_slot(slot, carry):
        frame, before_is_text = carry
        pos = slot * FT
        here = jnp.minimum(frame, frames - 1)
        is_frame = (frame < frames) & (vis_pos_ref[here] == pos)
        owner = slot // slots_each
        second = lax.rem(slot, slots_each) != 0
        partner = lax.rem(owner + peers // 2, peers)
        holder = jnp.where(second & (before_is_text == 1), partner, owner)
        source = jnp.where(is_frame, frame_host_ref[here], holder)
        flag = jnp.where(is_frame, 1, 0)
        place_ref[block_from(source) + peers * flag] = pos
        return frame + flag, 1 - flag

    lax.fori_loop(0, peers * slots_each, one_slot, (jnp.int32(0), jnp.int32(0)))


def tables(device, vis_pos, frame_host, doc_ids, peers, per_device):
    scalars = pl.BlockSpec(memory_space=pltpu.SMEM)
    return pl.pallas_call(
        functools.partial(tables_kernel, peers=peers, per_device=per_device),
        in_specs=[scalars] * 3 + [pl.BlockSpec(memory_space=pltpu.VMEM)],
        out_specs=scalars,
        out_shape=jax.ShapeDtypeStruct((2 * peers + DOCS,), jnp.int32),
    )(jnp.reshape(device, (1,)), vis_pos, frame_host, doc_ids.reshape(-1, LANES))


def attend_kernel(place_ref, q_ref, *rest, slots, heads):
    slot_refs, out_ref = rest[:slots], rest[slots]
    kv_ref, held_q_ref, query_ref, bias_ref, score_ref, max_ref, acc_ref, result_ref = rest[
        slots + 1 : slots + 9
    ]
    slot_sems, query_sems, out_sems = rest[slots + 9 :]
    rows = q_ref.shape[0]
    scale = 1.0 / math.sqrt(HD)
    wide = GROUP * HD
    first_pos = place_ref[slots]
    starts = [place_ref[slots + i] for i in range(1, DOCS)]

    def first_key(pos):
        return functools.reduce(jnp.maximum, [jnp.where(s <= pos, s, 0) for s in starts])

    last = first_pos // rows
    first = first_key(first_pos) // rows
    paired = first + (last - first) % 2
    masked_pairs = (jnp.maximum(first_key(first_pos + rows - 1) - paired * rows, 0) + 2 * rows - 1) // (
        2 * rows
    )
    pairs = (last - paired) // 2
    masked_pairs = jnp.minimum(masked_pairs, pairs)

    cuts = [(0, heads)]

    def slot_copy(i, cut):
        begin, end = cuts[cut]
        lanes = slice(begin * 2 * HD, end * 2 * HD)
        there = pl.ds(pl.multiple_of(place_ref[i], FT), FT)
        return pltpu.make_async_copy(
            slot_refs[i].at[:, lanes], kv_ref.at[there, lanes], slot_sems.at[cut, i]
        )

    def query_copy(cut):
        begin, end = cuts[cut]
        lanes = slice(begin * wide, end * wide)
        return pltpu.make_async_copy(
            q_ref.at[:, lanes], held_q_ref.at[:, lanes], query_sems.at[cut]
        )

    def wanted(i):
        block = place_ref[i] // rows
        return (block >= first) & (block <= last)

    def all_slots(cut, act):
        for i in range(slots):
            pl.when(wanted(i))(functools.partial(act, i, cut))

    for cut in range(len(cuts)):
        query_copy(cut).start()
        all_slots(cut, lambda i, cut: slot_copy(i, cut).start())

    def mask(block):
        query_pos = first_pos + lax.broadcasted_iota(jnp.int32, (rows, FT), 0)
        low = first_key(query_pos)
        for at in range(0, rows, FT):
            key_pos = block * rows + at + lax.broadcasted_iota(jnp.int32, (rows, FT), 1)
            allowed = (key_pos <= query_pos) & (key_pos >= low)
            bias_ref[block, :, at : at + FT] = jnp.where(allowed, 0.0, MASKED)

    pl.loop(first, paired + 2 * masked_pairs)(mask)
    mask(last)

    def result_copy(h):
        return pltpu.make_async_copy(
            result_ref.at[h], out_ref.at[:, h * wide : (h + 1) * wide], out_sems.at[h]
        )

    for cut in range(len(cuts)):
        query_copy(cut).wait()
        all_slots(cut, lambda i, cut: slot_copy(i, cut).wait())
    for h in range(heads):
        for g in range(GROUP):
            at = h * wide + g * HD
            query_ref[h, g * rows : (g + 1) * rows] = held_q_ref[:, at : at + HD]

    def score(block, count, masked, initial):
        here = pl.ds(pl.multiple_of(block * rows, rows), count * rows)
        for h in range(heads):
            keys = kv_ref[here, 2 * h * HD : (2 * h + 1) * HD]
            scores = contract_last(query_ref[h], keys) * scale
            parts = []
            for i in range(count):
                part = scores[:, i * rows : (i + 1) * rows]
                if masked:
                    part = part.reshape(GROUP, rows, rows) + bias_ref[block + i][None]
                    part = part.reshape(GROUP * rows, rows)
                score_ref[h, block + i] = part
                parts += [part[:, at : at + FT] for at in range(0, rows, FT)]
            if not initial:
                parts.append(max_ref[h])
            max_ref[h] = functools.reduce(jnp.maximum, parts)

    def mix(block, count, initial):
        here = pl.ds(pl.multiple_of(block * rows, rows), count * rows)
        for h in range(heads):
            values = kv_ref[here, (2 * h + 1) * HD : (2 * h + 2) * HD]
            values = jnp.concatenate([values, jnp.ones_like(values)], axis=1)
            weights = [
                jnp.exp(score_ref[h, block + i, :, at : at + FT] - max_ref[h]).astype(jnp.bfloat16)
                for i in range(count)
                for at in range(0, rows, FT)
            ]
            weights = jnp.concatenate(weights, axis=1)
            mixed = jnp.dot(weights, values, preferred_element_type=jnp.float32)
            acc_ref[h] = mixed if initial else acc_ref[h] + mixed

    score(last, 1, masked=True, initial=True)

    @pl.when(paired > first)
    def _():
        score(first, 1, masked=True, initial=False)

    @pl.loop(0, masked_pairs)
    def _(pair):
        score(paired + 2 * pair, 2, masked=True, initial=False)

    @pl.loop(masked_pairs, pairs)
    def _(pair):
        score(paired + 2 * pair, 2, masked=False, initial=False)

    for h in range(heads):
        row_max = jnp.max(max_ref[h], axis=1, keepdims=True)
        max_ref[h] = jnp.broadcast_to(row_max, (GROUP * rows, FT))

    mix(last, 1, initial=True)

    @pl.when(paired > first)
    def _():
        mix(first, 1, initial=False)

    @pl.loop(0, pairs)
    def _(pair):
        mix(paired + 2 * pair, 2, initial=False)

    for h in range(heads):
        mixed = acc_ref[h, :, :HD] / acc_ref[h, :, HD:]
        for g in range(GROUP):
            result_ref[h, :, g * HD : (g + 1) * HD] = mixed[g * rows : (g + 1) * rows].astype(
                result_ref.dtype
            )
        result_copy(h).start()
    for h in range(heads):
        result_copy(h).wait()


def attend(queries, slots, place):
    rows = queries.shape[0]
    columns = slots[0].shape[1]
    heads = columns // (2 * HD)
    blocks = len(slots) * FT // rows
    wide = GROUP * HD
    tall = GROUP * rows
    anywhere = pl.BlockSpec(memory_space=pl.ANY)
    scalars = pl.BlockSpec(memory_space=pltpu.SMEM)
    cells = heads * tall * blocks * rows
    return pl.pallas_call(
        functools.partial(attend_kernel, slots=len(slots), heads=heads),
        in_specs=[scalars] + [anywhere] * (1 + len(slots)),
        out_specs=anywhere,
        out_shape=jax.ShapeDtypeStruct(queries.shape, jnp.bfloat16),
        scratch_shapes=[
            pltpu.VMEM((len(slots) * FT, columns), jnp.bfloat16),
            pltpu.VMEM(queries.shape, jnp.bfloat16),
            pltpu.VMEM((heads, tall, HD), jnp.bfloat16),
            pltpu.VMEM((blocks, rows, rows), jnp.float32),
            pltpu.VMEM((heads, blocks, tall, rows), jnp.float32),
            pltpu.VMEM((heads, tall, FT), jnp.float32),
            pltpu.VMEM((heads, tall, 2 * HD), jnp.float32),
            pltpu.VMEM((heads, rows, wide), jnp.bfloat16),
            pltpu.SemaphoreType.DMA((2, len(slots))),
            pltpu.SemaphoreType.DMA((2,)),
            pltpu.SemaphoreType.DMA((heads,)),
        ],
        compiler_params=pltpu.CompilerParams(vmem_limit_bytes=LANGUAGE_VMEM),
        cost_estimate=pl.CostEstimate(
            flops=6 * cells * HD,
            bytes_accessed=2 * len(slots) * FT * columns + 4 * rows * heads * wide,
            transcendentals=cells,
        ),
    )(place, queries, *slots)


def shards(
    vis_qkv,
    vis_resid,
    vis_out_w,
    merge_gain,
    merge_bias,
    vis_kv_w,
    frame_host,
    vis_pos,
    doc_ids,
    text_kv,
    queries,
):
    device = lax.axis_index("ctx")
    tp_index = lax.axis_index("tp")
    tp_size = lax.axis_size("tp")
    per_device = queries.shape[0]
    patches = vis_qkv.shape[0]
    width = vis_qkv.shape[2]
    local_kv = vis_kv_w.shape[2] // tp_size
    positions = doc_ids.shape[0]
    frames = vis_pos.shape[0]

    peers = lax.axis_size("ctx")
    rows = peers // 2
    first_pos = device * per_device

    fields = jnp.transpose(vis_qkv, (1, 0, 2))
    part_count = 2
    part_rows = patches // part_count
    text_high = text_kv[FT:]
    handed = shifted(text_high, "ctx", peers // 2)
    (first_context,) = vit_attention(fields, text_high, 0, tp_index)
    second_context, low_rows, high_rows = vit_attention(
        fields, first_context, 1, tp_index, (first_context, vis_out_w, vis_resid)
    )
    contexts = [first_context, second_context]
    arrived = [
        [shifted(context, "tp", distance) for distance in range(1, tp_size)]
        for context in contexts
    ]

    def out_rows(distance):
        source = lax.rem(tp_after + tp_size - distance, tp_size)
        return lax.dynamic_slice_in_dim(vis_out_w, source * width, width, axis=0)

    vis_pos, text_kv, _ = lax.optimization_barrier((vis_pos, text_kv, second_context))
    first_frame = jnp.any(vis_pos == first_pos)
    second_frame = jnp.any(vis_pos == first_pos + FT)
    text_block = lax.dynamic_slice_in_dim(text_kv, jnp.where(first_frame, FT, 0), FT)
    handed, text_block, _ = lax.optimization_barrier((handed, text_block, low_rows))
    text_block = jnp.where(first_frame & second_frame, handed, text_block)
    hidden_parts = [low_rows, high_rows]
    text = Ring(text_block, rows)
    tp_after = tp_index
    for part in range(part_count):
        for distance in range(1, tp_size):
            hidden_parts[part] = hidden_parts[part] + jnp.dot(
                arrived[part][distance - 1], out_rows(distance), preferred_element_type=jnp.float32
            )
        if part == 0:
            tp_after, _ = lax.optimization_barrier((tp_index, hidden_parts[0]))
    hidden = jnp.concatenate(hidden_parts, axis=0)
    sums = jnp.stack([jnp.sum(hidden, axis=1), jnp.sum(hidden * hidden, axis=1)])
    others = [shifted(sums, "tp", distance) for distance in range(1, tp_size)]
    sums = text.advance(sums)
    row_sum, row_squares = functools.reduce(jnp.add, others, sums)
    mean_value = row_sum / VD
    variance = row_squares / VD - mean_value * mean_value
    normed = (hidden - mean_value[:, None]) * lax.rsqrt(variance + 1e-06)[
        :, None
    ] * merge_gain + merge_bias
    normed = normed.astype(jnp.bfloat16)

    received = []
    for distance in range(1, tp_size):
        block = lax.rem(tp_index + distance, tp_size)
        part = merged_columns(normed, vis_kv_w, block, local_kv, jnp.bfloat16)
        received.append(shifted(part, "tp", distance))
    own = merged_columns(normed, vis_kv_w, tp_index, local_kv, jnp.float32)
    own = text.advance(own)
    for part in received:
        own = own + part.astype(jnp.float32)
    own = own.astype(jnp.bfloat16)
    vision = Ring(own, rows)
    vis_pos, own = lax.optimization_barrier((vis_pos, own))
    place = tables(device, vis_pos, frame_host, doc_ids, peers, per_device)
    def laid(blocks, beside):
        come, _ = lax.optimization_barrier((blocks, beside))
        return [block.reshape(FT, local_kv) for block in come]

    texts, fresh = [], []
    for hop in range(1, rows):
        if hop == 1:
            vision.moving, place = text.advance((vision.moving, place))
        fresh = vision.advance(fresh, lag=1)
        texts += fresh
        ready = 2 * rows - 1 if hop > 1 else min(4, 2 * rows - 1)
        fresh = laid(text.blocks[len(texts) : ready], vision.blocks[-2])
    texts += fresh
    texts += laid(text.all()[len(texts) :], vision.blocks[-2])
    return attend(queries, texts + vision.all(), place)


def solution(mesh):
    return jax.shard_map(
        shards,
        mesh=mesh,
        in_specs=(
            P(("dp", "ctx"), None, "tp"),
            P(("dp", "ctx"), "tp"),
            P(None, "tp"),
            P("tp"),
            P("tp"),
            P(None, "tp", None),
            P("dp"),
            P("dp"),
            P("dp"),
            P(("dp", "ctx"), "tp", None, None),
            P(("dp", "ctx"), "tp"),
        ),
        out_specs=P(("dp", "ctx"), "tp"),
        check_vma=False,
    )
```

profile of v0, /device:TPU:22, one launch (start us, length us, event | category | flops | bytes accessed | tf_op | source)
XLA Modules:
  0.0 88.0 jit_solution(18092607073197187112)
XLA Ops:
  0.0 1.1 %slice.3.after_ref = bf16[128,4,2,128]{3,2,1,0:T(2,128)(2,1)S(1)} slice(bf16[256,4,2,128]{3,2,1,0:T(2,128)(2,1)} %param.20), slice={[128:256], [0:4], [0:2], [0:128]} | slice | bytes 524288 | tf_op jit(solution)/shard_map/slice | solution.py:470
  1.5 1.5 %copy-done = bf16[512,3,640]{2,0,1:T(8,128)(2,1)S(1)} copy-done((bf16[512,3,640]{2,0,1:T(8,128)(2,1)S(1)}, bf16[512,3,640]{2,0,1:T(8,128)(2,1)}, u32[]{:S(2)}) %copy-start) | copy-done | bytes 1966104
  3.1 2.1 %shard_map.109.after_ref.rest_0_ = bf16[256,640]{1,0:T(8,128)(2,1)S(1)} custom-call(s32[1]{0:T(128)} %bitcast.index_ref.block_ref, bf16[3,512,640]{2,1,0:T(8,128)(2,1)S(1)} %bitcast.14, bf16[3,512,640]{2,1,0:T(8,128)(2,1)S(1)} %bitcast.15, bf16[3,512,640]{2,1,0:T(8,128)(2,1)S(1)} %bitcast.16, bf16[128,4,2,128]{3,2,1,0:T(2,128)(2,1)S(1)} %slice.3.after_ref), custom_call_target="tpu_custom_call" | custom-call | flops 1024 | bytes 1024 | tf_op jit(solution)/shard_map/pallas_call | solution.py:147
  5.8 2.9 %shard_map.110 = (bf16[256,640]{1,0:T(8,128)(2,1)}, f32[256,640]{1,0:T(8,128)S(1)}, f32[256,640]{1,0:T(8,128)S(1)}) custom-call(s32[1]{0:T(128)} %bitcast.index_ref.block_ref, bf16[3,512,640]{2,1,0:T(8,128)(2,1)S(1)} %bitcast.17, bf16[3,512,640]{2,1,0:T(8,128)(2,1)S(1)} %bitcast.18, bf16[3,512,640]{2,1,0:T(8,128)(2,1)S(1)} %bitcast.19, ...), custom_call_target="tpu_custom_call" | custom-call | flops 1024 | bytes 1024 | tf_op jit(solution)/shard_map/pallas_call | solution.py:147
  8.7 1.5 %collective-permute-start.4 = (bf16[256,640]{1,0:T(8,128)(2,1)}, bf16[256,640]{1,0:T(8,128)(2,1)}, u32[]{:S(2)}, u32[]{:S(2)}) collective-permute-start(bf16[256,640]{1,0:T(8,128)(2,1)} %get-tuple-element.43), channel_id=1, source_target_pairs={{0,2},{2,0},{1,3},{3,1},{4,6},{6,4},{5,7},{7,5},{8,10},{10,8},{9,1... | collective-permute-start | bytes 983048 | tf_op jit(solution)/shard_map/ppermute | solution.py:33
  12.8 1.1 %constant_dynamic-slice_fusion = bf16[128,4,2,128]{3,2,1,0:T(2,128)(2,1)S(1)} fusion(bf16[256,4,2,128]{3,2,1,0:T(2,128)(2,1)} %param.20, s32[]{:T(128)S(6)} %select_n.20), kind=kLoop, calls=%fused_computation.18 | loop fusion | bytes 524292 | tf_op jit(solution)/shard_map/dynamic_slice | solution.py:489
  14.6 3.5 %collective-permute-start.1 = (bf16[128,4,2,128]{3,2,1,0:T(2,128)(2,1)S(1)}, bf16[128,4,2,128]{3,2,1,0:T(2,128)(2,1)}, u32[]{:S(2)}, u32[]{:S(2)}) collective-permute-start(bf16[128,4,2,128]{3,2,1,0:T(2,128)(2,1)S(1)} %bitcast.22), channel_id=1, source_target_pairs={{0,8},{4,12},{8,24},{12,28},{16,0},{20,4},{24,16},{28,20},{1,9},{5... | collective-permute-start | bytes 786440 | tf_op jit(solution)/shard_map/ppermute | solution.py:43
  18.2 2.3 %convolution_add_fusion.1 = f32[256,640]{1,0:T(8,128)} fusion(f32[256,640]{1,0:T(8,128)S(1)} %get-tuple-element.46, bf16[256,640]{1,0:T(8,128)(2,1)} %collective-permute-done.3, bf16[1280,640]{1,0:T(8,128)(2,1)S(1)} %copy-done.1, s32[]{:T(128)S(6)} %select_n.22), kind=kOutput, calls=%fused_computation.4 | convolution fusion | flops 209879040 | bytes 2457604 | tf_op jit(solution)/shard_map/dot_general | solution.py:497
  20.4 1.2 %collective-permute-done.4 = bf16[256,640]{1,0:T(8,128)(2,1)} collective-permute-done((bf16[256,640]{1,0:T(8,128)(2,1)}, bf16[256,640]{1,0:T(8,128)(2,1)}, u32[]{:S(2)}, u32[]{:S(2)}) %collective-permute-start.4) | collective-permute-done | bytes 327712 | tf_op jit(solution)/shard_map/ppermute | solution.py:33
  21.6 1.5 %convolution_add_fusion = f32[256,640]{1,0:T(8,128)S(1)} fusion(f32[256,640]{1,0:T(8,128)S(1)} %get-tuple-element.49, bf16[256,640]{1,0:T(8,128)(2,1)} %collective-permute-done.4, bf16[1280,640]{1,0:T(8,128)(2,1)S(1)} %copy-done.1, s32[]{:T(128)S(6)} %select_n.23), kind=kOutput, calls=%fused_computation.3 | convolution fusion | flops 209879040 | bytes 2457604 | tf_op jit(solution)/shard_map/dot_general | solution.py:497
  24.0 1.1 %collective-permute-done.1 = bf16[128,4,2,128]{3,2,1,0:T(2,128)(2,1)} collective-permute-done((bf16[128,4,2,128]{3,2,1,0:T(2,128)(2,1)S(1)}, bf16[128,4,2,128]{3,2,1,0:T(2,128)(2,1)}, u32[]{:S(2)}, u32[]{:S(2)}) %collective-permute-start.1) | collective-permute-done | bytes 262176 | tf_op jit(solution)/shard_map/ppermute | solution.py:43
  25.1 1.7 %collective-permute-start.6 = (bf16[128,4,2,128]{3,2,1,0:T(2,128)(2,1)}, bf16[128,4,2,128]{3,2,1,0:T(2,128)(2,1)S(1)}, u32[]{:S(2)}, u32[]{:S(2)}) collective-permute-start(bf16[128,4,2,128]{3,2,1,0:T(2,128)(2,1)} %collective-permute-done.1), channel_id=1, source_target_pairs={{0,4},{4,0},{8,12},{12,8},{16,20},{20,16},{24,28},{28,24},{1,5},{5... | collective-permute-start | bytes 786440 | tf_op jit(solution)/shard_map/ppermute | solution.py:51
  27.4 2.9 %shard_map.112 = bf16[128,1024]{1,0:T(8,128)(2,1)S(1)} custom-call(s32[1]{0:T(128)} %bitcast.6.block_ref, bf16[512,640]{1,0:T(8,128)(2,1)S(1)} %add_convert_fusion.x_ref, bf16[4,640,2048]{2,1,0:T(8,128)(2,1)} %w_ref.3), custom_call_target="tpu_custom_call" | custom-call | flops 671088640 | bytes 5898240 | tf_op jit(solution)/shard_map/pallas_call | solution.py:188
  30.3 1.6 %collective-permute-start.10 = (bf16[128,1024]{1,0:T(8,128)(2,1)S(1)}, bf16[128,1024]{1,0:T(8,128)(2,1)S(1)}, u32[]{:S(2)}, u32[]{:S(2)}) collective-permute-start(bf16[128,1024]{1,0:T(8,128)(2,1)S(1)} %shard_map.112), channel_id=1, source_target_pairs={{0,2},{2,0},{1,3},{3,1},{4,6},{6,4},{5,7},{7,5},{8,10},{10,8},{9,1... | collective-permute-start | bytes 786440 | tf_op jit(solution)/shard_map/ppermute | solution.py:33
  31.9 2.9 %shard_map.111 = f32[128,1024]{1,0:T(8,128)S(1)} custom-call(s32[1]{0:T(128)} %bitcast.index_ref.block_ref, bf16[512,640]{1,0:T(8,128)(2,1)S(1)} %add_convert_fusion.x_ref, bf16[4,640,2048]{2,1,0:T(8,128)(2,1)} %w_ref.3), custom_call_target="tpu_custom_call" | custom-call | flops 671088640 | bytes 5898240 | tf_op jit(solution)/shard_map/pallas_call | solution.py:188
  35.6 2.5 %collective-permute-done.10 = bf16[128,1024]{1,0:T(8,128)(2,1)S(1)} collective-permute-done((bf16[128,1024]{1,0:T(8,128)(2,1)S(1)}, bf16[128,1024]{1,0:T(8,128)(2,1)S(1)}, u32[]{:S(2)}, u32[]{:S(2)}) %collective-permute-start.10) | collective-permute-done | bytes 262176 | tf_op jit(solution)/shard_map/ppermute | solution.py:33
  38.2 1.6 %collective-permute-start.11 = (bf16[128,1024]{1,0:T(8,128)(2,1)S(1)}, bf16[128,1024]{1,0:T(8,128)(2,1)S(1)}, u32[]{:S(2)}, u32[]{:S(2)}) collective-permute-start(bf16[128,1024]{1,0:T(8,128)(2,1)S(1)} %add_convert_fusion.1.rest_8_), channel_id=1, source_target_pairs={{0,8},{4,12},{8,24},{12,28},{16,0},{20,4},{24,16},{28,20},{1,9},{5... | collective-permute-start | bytes 786440 | tf_op jit(solution)/shard_map/ppermute | solution.py:43
  40.0 3.5 %collective-permute-start.8 = (bf16[128,4,2,128]{3,2,1,0:T(2,128)(2,1)S(1)}, bf16[128,4,2,128]{3,2,1,0:T(2,128)(2,1)S(1)}, u32[]{:S(2)}, u32[]{:S(2)}) collective-permute-start(bf16[128,4,2,128]{3,2,1,0:T(2,128)(2,1)S(1)} %collective-permute-done.5), channel_id=1, source_target_pairs={{0,8},{4,12},{8,24},{12,28},{16,0},{20,4},{24,16},{28,20},{1,9},{5... | collective-permute-start | bytes 786440 | tf_op jit(solution)/shard_map/ppermute | solution.py:43
  43.5 1.7 %collective-permute-start.13 = (bf16[128,1024]{1,0:T(8,128)(2,1)S(1)}, bf16[128,1024]{1,0:T(8,128)(2,1)S(1)}, u32[]{:S(2)}, u32[]{:S(2)}) collective-permute-start(bf16[128,1024]{1,0:T(8,128)(2,1)S(1)} %add_convert_fusion.1.rest_8_), channel_id=1, source_target_pairs={{0,4},{4,0},{8,12},{12,8},{16,20},{20,16},{24,28},{28,24},{1,5},{5... | collective-permute-start | bytes 786440 | tf_op jit(solution)/shard_map/ppermute | solution.py:51
  45.3 2.2 %shard_map.113.place_ref = s32[20]{0:T(128)} custom-call(s32[1]{0:T(128)} %bitcast.7.device_ref, s32[8]{0:T(128)} %vis_pos_ref, s32[8]{0:T(128)} %frame_host_ref.1, s32[16,128]{1,0:T(8,128)} %bitcast.28), custom_call_target="tpu_custom_call" | custom-call | tf_op jit(solution)/shard_map/pallas_call | solution.py:248
  48.6 2.7 %collective-permute-done.8 = bf16[128,4,2,128]{3,2,1,0:T(2,128)(2,1)S(1)} collective-permute-done((bf16[128,4,2,128]{3,2,1,0:T(2,128)(2,1)S(1)}, bf16[128,4,2,128]{3,2,1,0:T(2,128)(2,1)S(1)}, u32[]{:S(2)}, u32[]{:S(2)}) %collective-permute-start.8) | collective-permute-done | bytes 262176 | tf_op jit(solution)/shard_map/ppermute | solution.py:43
  51.3 1.6 %collective-permute-start.12 = (bf16[128,1024]{1,0:T(8,128)(2,1)S(1)}, bf16[128,1024]{1,0:T(8,128)(2,1)S(1)}, u32[]{:S(2)}, u32[]{:S(2)}) collective-permute-start(bf16[128,1024]{1,0:T(8,128)(2,1)S(1)} %collective-permute-done.11.rest_10_), channel_id=1, source_target_pairs={{0,8},{4,12},{8,24},{12,28},{16,0},{20,4},{24,16},{28,20},{1,9},{5... | collective-permute-start | bytes 786440 | tf_op jit(solution)/shard_map/ppermute | solution.py:43
  54.0 1.8 %reshape.66.rest_1_ = bf16[128,1024]{1,0:T(8,128)(2,1)} reshape(bf16[128,4,2,128]{3,2,1,0:T(2,128)(2,1)} %collective-permute-done.2) | data formatting | bytes 524288 | tf_op jit(solution)/shard_map/reshape | solution.py:529
  55.8 1.8 %reshape.67.rest_2_ = bf16[128,1024]{1,0:T(8,128)(2,1)} reshape(bf16[128,4,2,128]{3,2,1,0:T(2,128)(2,1)} %collective-permute-done.1) | data formatting | bytes 524288 | tf_op jit(solution)/shard_map/reshape | solution.py:529
  58.5 2.7 %collective-permute-start.14 = (bf16[128,1024]{1,0:T(8,128)(2,1)S(1)}, bf16[128,1024]{1,0:T(8,128)(2,1)S(1)}, u32[]{:S(2)}, u32[]{:S(2)}) collective-permute-start(bf16[128,1024]{1,0:T(8,128)(2,1)S(1)} %collective-permute-done.12.rest_12_), channel_id=1, source_target_pairs={{0,8},{4,12},{8,24},{12,28},{16,0},{20,4},{24,16},{28,20},{1,9},{5... | collective-permute-start | bytes 786440 | tf_op jit(solution)/shard_map/ppermute | solution.py:43
  61.3 1.8 %collective-permute-start.16 = (bf16[128,4,2,128]{3,2,1,0:T(2,128)(2,1)S(1)}, bf16[128,4,2,128]{3,2,1,0:T(2,128)(2,1)S(1)}, u32[]{:S(2)}, u32[]{:S(2)}) collective-permute-start(bf16[128,4,2,128]{3,2,1,0:T(2,128)(2,1)S(1)} %collective-permute-done.8), channel_id=1, source_target_pairs={{0,4},{4,0},{8,12},{12,8},{16,20},{20,16},{24,28},{28,24},{1,5},{5... | collective-permute-start | bytes 786440 | tf_op jit(solution)/shard_map/ppermute | solution.py:51
  63.3 0.9 %reshape.69.rest_4_ = bf16[128,1024]{1,0:T(8,128)(2,1)} reshape(bf16[128,4,2,128]{3,2,1,0:T(2,128)(2,1)S(1)} %collective-permute-done.5) | data formatting | bytes 524288 | tf_op jit(solution)/shard_map/reshape | solution.py:529
  66.0 1.9 %collective-permute-start.18 = (bf16[128,1024]{1,0:T(8,128)(2,1)S(1)}, bf16[128,1024]{1,0:T(8,128)(2,1)S(1)}, u32[]{:S(2)}, u32[]{:S(2)}) collective-permute-start(bf16[128,1024]{1,0:T(8,128)(2,1)S(1)} %collective-permute-done.14.rest_14_), channel_id=1, source_target_pairs={{0,4},{4,0},{8,12},{12,8},{16,20},{20,16},{24,28},{28,24},{1,5},{5... | collective-permute-start | bytes 786440 | tf_op jit(solution)/shard_map/ppermute | solution.py:51
  67.8 2.7 %collective-permute-done.16 = bf16[128,4,2,128]{3,2,1,0:T(2,128)(2,1)S(1)} collective-permute-done((bf16[128,4,2,128]{3,2,1,0:T(2,128)(2,1)S(1)}, bf16[128,4,2,128]{3,2,1,0:T(2,128)(2,1)S(1)}, u32[]{:S(2)}, u32[]{:S(2)}) %collective-permute-start.16) | collective-permute-done | bytes 262176 | tf_op jit(solution)/shard_map/ppermute | solution.py:51
  71.4 3.2 %collective-permute-done.17.rest_13_ = bf16[128,1024]{1,0:T(8,128)(2,1)S(1)} collective-permute-done((bf16[128,1024]{1,0:T(8,128)(2,1)S(1)}, bf16[128,1024]{1,0:T(8,128)(2,1)S(1)}, u32[]{:S(2)}, u32[]{:S(2)}) %collective-permute-start.17) | collective-permute-done | bytes 262176 | tf_op jit(solution)/shard_map/ppermute | solution.py:51
  74.5 2.8 %collective-permute-done.18.rest_15_ = bf16[128,1024]{1,0:T(8,128)(2,1)S(1)} collective-permute-done((bf16[128,1024]{1,0:T(8,128)(2,1)S(1)}, bf16[128,1024]{1,0:T(8,128)(2,1)S(1)}, u32[]{:S(2)}, u32[]{:S(2)}) %collective-permute-start.18) | collective-permute-done | bytes 262176 | tf_op jit(solution)/shard_map/ppermute | solution.py:51
  78.1 9.7 %shard_map.114 = bf16[256,2048]{1,0:T(8,128)(2,1)} custom-call(s32[20]{0:T(128)} %shard_map.113.place_ref, bf16[256,2048]{1,0:T(8,128)(2,1)} %q_ref.1, bf16[128,1024]{1,0:T(8,128)(2,1)} %reshape.65.rest_0_, bf16[128,1024]{1,0:T(8,128)(2,1)} %reshape.66.rest_1_, bf16[128,1024]{1,0:T(8,128)(2,1)} %reshape.67.rest_2_, bf16[128,1024]{1,0:T(8,128)(2,1)} %reshape.68.rest_3_, ...), custom_call_target="tpu_custom_call" | custom-call | flops 6442450944 | bytes 6291456 | tf_op jit(solution)/shard_map/pallas_call | solution.py:413
  (63 shorter events, 11.7 us)
Async XLA Ops:
  1.1 12.8 %collective-permute-start = (bf16[128,4,2,128]{3,2,1,0:T(2,128)(2,1)S(1)}, bf16[128,4,2,128]{3,2,1,0:T(2,128)(2,1)}, u32[]{:S(2)}, u32[]{:S(2)}) collective-permute-start(bf16[128,4,2,128]{3,2,1,0:T(2,128)(2,1)S(1)} %slice.3.after_ref), channel_id=1, source_target_pairs={{0,16},{4,20},{8,24},{12,28},{16,0},{20,4},{24,8},{28,12},{1,17},{... | collective-permute-start | bytes 786440 | tf_op jit(solution)/shard_map/ppermute | solution.py:33
  3.1 2.7 %copy-start.1 = (bf16[1280,640]{1,0:T(8,128)(2,1)S(1)}, bf16[1280,640]{1,0:T(8,128)(2,1)}, u32[]{:S(2)}) copy-start(bf16[1280,640]{1,0:T(8,128)(2,1)} %rest_1_.1) | copy-start | bytes 4915204
  3.1 2.7 %copy-start.2 = (bf16[512,640]{1,0:T(8,128)(2,1)S(1)}, bf16[512,640]{1,0:T(8,128)(2,1)}, u32[]{:S(2)}) copy-start(bf16[512,640]{1,0:T(8,128)(2,1)} %rest_2_.1) | copy-start | bytes 1966084
  5.2 5.0 %copy-start.7 = (s32[8]{0:T(128)S(1)}, s32[8]{0:T(128)}, u32[]{:S(2)}) copy-start(s32[8]{0:T(128)} %vis_pos_ref) | copy-start | bytes 100
  5.2 12.9 %collective-permute-start.3 = (bf16[256,640]{1,0:T(8,128)(2,1)S(1)}, bf16[256,640]{1,0:T(8,128)(2,1)}, u32[]{:S(2)}, u32[]{:S(2)}) collective-permute-start(bf16[256,640]{1,0:T(8,128)(2,1)S(1)} %shard_map.109.after_ref.rest_0_), channel_id=1, source_target_pairs={{0,2},{2,0},{1,3},{3,1},{4,6},{6,4},{5,7},{7,5},{8,10},{10,8},{9,1... | collective-permute-start | bytes 983048 | tf_op jit(solution)/shard_map/ppermute | solution.py:33
  8.7 12.9 %collective-permute-start.4 = (bf16[256,640]{1,0:T(8,128)(2,1)}, bf16[256,640]{1,0:T(8,128)(2,1)}, u32[]{:S(2)}, u32[]{:S(2)}) collective-permute-start(bf16[256,640]{1,0:T(8,128)(2,1)} %get-tuple-element.43), channel_id=1, source_target_pairs={{0,2},{2,0},{1,3},{3,1},{4,6},{6,4},{5,7},{7,5},{8,10},{10,8},{9,1... | collective-permute-start | bytes 983048 | tf_op jit(solution)/shard_map/ppermute | solution.py:33
  14.0 9.9 %collective-permute-start.2 = (bf16[128,4,2,128]{3,2,1,0:T(2,128)(2,1)S(1)}, bf16[128,4,2,128]{3,2,1,0:T(2,128)(2,1)}, u32[]{:S(2)}, u32[]{:S(2)}) collective-permute-start(bf16[128,4,2,128]{3,2,1,0:T(2,128)(2,1)S(1)} %bitcast.21), channel_id=1, source_target_pairs={{0,4},{4,0},{8,12},{12,8},{16,20},{20,16},{24,28},{28,24},{1,5},{5... | collective-permute-start | bytes 786440 | tf_op jit(solution)/shard_map/ppermute | solution.py:51
  14.6 10.4 %collective-permute-start.1 = (bf16[128,4,2,128]{3,2,1,0:T(2,128)(2,1)S(1)}, bf16[128,4,2,128]{3,2,1,0:T(2,128)(2,1)}, u32[]{:S(2)}, u32[]{:S(2)}) collective-permute-start(bf16[128,4,2,128]{3,2,1,0:T(2,128)(2,1)S(1)} %bitcast.22), channel_id=1, source_target_pairs={{0,8},{4,12},{8,24},{12,28},{16,0},{20,4},{24,16},{28,20},{1,9},{5... | collective-permute-start | bytes 786440 | tf_op jit(solution)/shard_map/ppermute | solution.py:43
  20.4 2.6 %copy-start.3 = (f32[256,640]{1,0:T(8,128)S(1)}, f32[256,640]{1,0:T(8,128)}, u32[]{:S(2)}) copy-start(f32[256,640]{1,0:T(8,128)} %convolution_add_fusion.1) | copy-start | bytes 1966084
  21.6 5.5 %copy-start.5 = (f32[640]{0:T(1024)S(1)}, f32[640]{0:T(1024)}, u32[]{:S(2)}) copy-start(f32[640]{0:T(1024)} %param.15) | copy-start | bytes 7684
  21.6 5.5 %copy-start.6 = (f32[640]{0:T(1024)S(1)}, f32[640]{0:T(1024)}, u32[]{:S(2)}) copy-start(f32[640]{0:T(1024)} %param.14) | copy-start | bytes 7684
  23.4 3.7 %collective-permute-start.7 = (f32[2,512]{1,0:T(2,128)S(1)}, f32[2,512]{1,0:T(2,128)S(1)}, u32[]{:S(2)}, u32[]{:S(2)}) collective-permute-start(f32[2,512]{1,0:T(2,128)S(1)} %pad_maximum_fusion.1), channel_id=1, source_target_pairs={{0,2},{2,0},{1,3},{3,1},{4,6},{6,4},{5,7},{7,5},{8,10},{10,8},{9,1... | collective-permute-start | bytes 12296 | tf_op jit(solution)/shard_map/ppermute | solution.py:33
  25.1 9.8 %collective-permute-start.6 = (bf16[128,4,2,128]{3,2,1,0:T(2,128)(2,1)}, bf16[128,4,2,128]{3,2,1,0:T(2,128)(2,1)S(1)}, u32[]{:S(2)}, u32[]{:S(2)}) collective-permute-start(bf16[128,4,2,128]{3,2,1,0:T(2,128)(2,1)} %collective-permute-done.1), channel_id=1, source_target_pairs={{0,4},{4,0},{8,12},{12,8},{16,20},{20,16},{24,28},{28,24},{1,5},{5... | collective-permute-start | bytes 786440 | tf_op jit(solution)/shard_map/ppermute | solution.py:51
  26.7 8.9 %collective-permute-start.5 = (bf16[128,4,2,128]{3,2,1,0:T(2,128)(2,1)}, bf16[128,4,2,128]{3,2,1,0:T(2,128)(2,1)S(1)}, u32[]{:S(2)}, u32[]{:S(2)}) collective-permute-start(bf16[128,4,2,128]{3,2,1,0:T(2,128)(2,1)} %collective-permute-done.1), channel_id=1, source_target_pairs={{0,8},{4,12},{8,24},{12,28},{16,0},{20,4},{24,16},{28,20},{1,9},{5... | collective-permute-start | bytes 786440 | tf_op jit(solution)/shard_map/ppermute | solution.py:43
  30.3 7.8 %collective-permute-start.10 = (bf16[128,1024]{1,0:T(8,128)(2,1)S(1)}, bf16[128,1024]{1,0:T(8,128)(2,1)S(1)}, u32[]{:S(2)}, u32[]{:S(2)}) collective-permute-start(bf16[128,1024]{1,0:T(8,128)(2,1)S(1)} %shard_map.112), channel_id=1, source_target_pairs={{0,2},{2,0},{1,3},{3,1},{4,6},{6,4},{5,7},{7,5},{8,10},{10,8},{9,1... | collective-permute-start | bytes 786440 | tf_op jit(solution)/shard_map/ppermute | solution.py:33
  38.2 26.0 %copy-start.4 = (bf16[128,1024]{1,0:T(8,128)(2,1)}, bf16[128,1024]{1,0:T(8,128)(2,1)S(1)}, u32[]{:S(2)}) copy-start(bf16[128,1024]{1,0:T(8,128)(2,1)S(1)} %add_convert_fusion.1.rest_8_) | copy-start | bytes 786436
  38.2 9.6 %collective-permute-start.11 = (bf16[128,1024]{1,0:T(8,128)(2,1)S(1)}, bf16[128,1024]{1,0:T(8,128)(2,1)S(1)}, u32[]{:S(2)}, u32[]{:S(2)}) collective-permute-start(bf16[128,1024]{1,0:T(8,128)(2,1)S(1)} %add_convert_fusion.1.rest_8_), channel_id=1, source_target_pairs={{0,8},{4,12},{8,24},{12,28},{16,0},{20,4},{24,16},{28,20},{1,9},{5... | collective-permute-start | bytes 786440 | tf_op jit(solution)/shard_map/ppermute | solution.py:43
  39.8 8.9 %collective-permute-start.9 = (bf16[128,4,2,128]{3,2,1,0:T(2,128)(2,1)S(1)}, bf16[128,4,2,128]{3,2,1,0:T(2,128)(2,1)S(1)}, u32[]{:S(2)}, u32[]{:S(2)}) collective-permute-start(bf16[128,4,2,128]{3,2,1,0:T(2,128)(2,1)S(1)} %collective-permute-done.5), channel_id=1, source_target_pairs={{0,4},{4,0},{8,12},{12,8},{16,20},{20,16},{24,28},{28,24},{1,5},{5... | collective-permute-start | bytes 786440 | tf_op jit(solution)/shard_map/ppermute | solution.py:51
  40.0 11.3 %collective-permute-start.8 = (bf16[128,4,2,128]{3,2,1,0:T(2,128)(2,1)S(1)}, bf16[128,4,2,128]{3,2,1,0:T(2,128)(2,1)S(1)}, u32[]{:S(2)}, u32[]{:S(2)}) collective-permute-start(bf16[128,4,2,128]{3,2,1,0:T(2,128)(2,1)S(1)} %collective-permute-done.5), channel_id=1, source_target_pairs={{0,8},{4,12},{8,24},{12,28},{16,0},{20,4},{24,16},{28,20},{1,9},{5... | collective-permute-start | bytes 786440 | tf_op jit(solution)/shard_map/ppermute | solution.py:43
  43.5 15.0 %collective-permute-start.13 = (bf16[128,1024]{1,0:T(8,128)(2,1)S(1)}, bf16[128,1024]{1,0:T(8,128)(2,1)S(1)}, u32[]{:S(2)}, u32[]{:S(2)}) collective-permute-start(bf16[128,1024]{1,0:T(8,128)(2,1)S(1)} %add_convert_fusion.1.rest_8_), channel_id=1, source_target_pairs={{0,4},{4,0},{8,12},{12,8},{16,20},{20,16},{24,28},{28,24},{1,5},{5... | collective-permute-start | bytes 786440 | tf_op jit(solution)/shard_map/ppermute | solution.py:51
  47.8 16.4 %copy-start.8 = (bf16[128,1024]{1,0:T(8,128)(2,1)}, bf16[128,1024]{1,0:T(8,128)(2,1)S(1)}, u32[]{:S(2)}) copy-start(bf16[128,1024]{1,0:T(8,128)(2,1)S(1)} %collective-permute-done.11.rest_10_) | copy-start | bytes 786436
  51.3 7.2 %collective-permute-start.12 = (bf16[128,1024]{1,0:T(8,128)(2,1)S(1)}, bf16[128,1024]{1,0:T(8,128)(2,1)S(1)}, u32[]{:S(2)}, u32[]{:S(2)}) collective-permute-start(bf16[128,1024]{1,0:T(8,128)(2,1)S(1)} %collective-permute-done.11.rest_10_), channel_id=1, source_target_pairs={{0,8},{4,12},{8,24},{12,28},{16,0},{20,4},{24,16},{28,20},{1,9},{5... | collective-permute-start | bytes 786440 | tf_op jit(solution)/shard_map/ppermute | solution.py:43
  52.9 13.0 %collective-permute-start.15 = (bf16[128,1024]{1,0:T(8,128)(2,1)S(1)}, bf16[128,1024]{1,0:T(8,128)(2,1)S(1)}, u32[]{:S(2)}, u32[]{:S(2)}) collective-permute-start(bf16[128,1024]{1,0:T(8,128)(2,1)S(1)} %collective-permute-done.11.rest_10_), channel_id=1, source_target_pairs={{0,4},{4,0},{8,12},{12,8},{16,20},{20,16},{24,28},{28,24},{1,5},{5... | collective-permute-start | bytes 786440 | tf_op jit(solution)/shard_map/ppermute | solution.py:51
  58.5 18.8 %copy-start.9 = (bf16[128,1024]{1,0:T(8,128)(2,1)}, bf16[128,1024]{1,0:T(8,128)(2,1)S(1)}, u32[]{:S(2)}) copy-start(bf16[128,1024]{1,0:T(8,128)(2,1)S(1)} %collective-permute-done.13.rest_9_) | copy-start | bytes 786436
  58.5 18.8 %copy-start.10 = (bf16[128,1024]{1,0:T(8,128)(2,1)}, bf16[128,1024]{1,0:T(8,128)(2,1)S(1)}, u32[]{:S(2)}) copy-start(bf16[128,1024]{1,0:T(8,128)(2,1)S(1)} %collective-permute-done.12.rest_12_) | copy-start | bytes 786436
  58.5 7.4 %collective-permute-start.14 = (bf16[128,1024]{1,0:T(8,128)(2,1)S(1)}, bf16[128,1024]{1,0:T(8,128)(2,1)S(1)}, u32[]{:S(2)}, u32[]{:S(2)}) collective-permute-start(bf16[128,1024]{1,0:T(8,128)(2,1)S(1)} %collective-permute-done.12.rest_12_), channel_id=1, source_target_pairs={{0,8},{4,12},{8,24},{12,28},{16,0},{20,4},{24,16},{28,20},{1,9},{5... | collective-permute-start | bytes 786440 | tf_op jit(solution)/shard_map/ppermute | solution.py:43
  61.3 9.2 %collective-permute-start.16 = (bf16[128,4,2,128]{3,2,1,0:T(2,128)(2,1)S(1)}, bf16[128,4,2,128]{3,2,1,0:T(2,128)(2,1)S(1)}, u32[]{:S(2)}, u32[]{:S(2)}) collective-permute-start(bf16[128,4,2,128]{3,2,1,0:T(2,128)(2,1)S(1)} %collective-permute-done.8), channel_id=1, source_target_pairs={{0,4},{4,0},{8,12},{12,8},{16,20},{20,16},{24,28},{28,24},{1,5},{5... | collective-permute-start | bytes 786440 | tf_op jit(solution)/shard_map/ppermute | solution.py:51
  63.1 11.5 %collective-permute-start.17 = (bf16[128,1024]{1,0:T(8,128)(2,1)S(1)}, bf16[128,1024]{1,0:T(8,128)(2,1)S(1)}, u32[]{:S(2)}, u32[]{:S(2)}) collective-permute-start(bf16[128,1024]{1,0:T(8,128)(2,1)S(1)} %collective-permute-done.12.rest_12_), channel_id=1, source_target_pairs={{0,4},{4,0},{8,12},{12,8},{16,20},{20,16},{24,28},{28,24},{1,5},{5... | collective-permute-start | bytes 786440 | tf_op jit(solution)/shard_map/ppermute | solution.py:51
  65.9 11.4 %copy-start.11 = (bf16[128,1024]{1,0:T(8,128)(2,1)}, bf16[128,1024]{1,0:T(8,128)(2,1)S(1)}, u32[]{:S(2)}) copy-start(bf16[128,1024]{1,0:T(8,128)(2,1)S(1)} %collective-permute-done.15.rest_11_) | copy-start | bytes 786436
  65.9 11.4 %copy-start.12 = (bf16[128,1024]{1,0:T(8,128)(2,1)}, bf16[128,1024]{1,0:T(8,128)(2,1)S(1)}, u32[]{:S(2)}) copy-start(bf16[128,1024]{1,0:T(8,128)(2,1)S(1)} %collective-permute-done.14.rest_14_) | copy-start | bytes 786436
  66.0 11.4 %collective-permute-start.18 = (bf16[128,1024]{1,0:T(8,128)(2,1)S(1)}, bf16[128,1024]{1,0:T(8,128)(2,1)S(1)}, u32[]{:S(2)}, u32[]{:S(2)}) collective-permute-start(bf16[128,1024]{1,0:T(8,128)(2,1)S(1)} %collective-permute-done.14.rest_14_), channel_id=1, source_target_pairs={{0,4},{4,0},{8,12},{12,8},{16,20},{20,16},{24,28},{28,24},{1,5},{5... | collective-permute-start | bytes 786440 | tf_op jit(solution)/shard_map/ppermute | solution.py:51
  74.5 2.8 %copy-start.13 = (bf16[128,1024]{1,0:T(8,128)(2,1)}, bf16[128,1024]{1,0:T(8,128)(2,1)S(1)}, u32[]{:S(2)}) copy-start(bf16[128,1024]{1,0:T(8,128)(2,1)S(1)} %collective-permute-done.17.rest_13_) | copy-start | bytes 786436
  (2 other events, 2.2 us)
where the time goes:
time: 88.6 us; the launch traced here: 88 us
  starting transfers between devices  26.3 us (30%)
  Pallas kernels  22.8 us (26%)
  waiting for transfers between devices  18.1 us (20%)
  local copies, waits for them, and re-layouts  13.4 us (15%)
  matrix products  3.72 us (4%)
  between operations  2.29 us (3%)
  other arithmetic  1.41 us (2%)
    ppermute x6, starting transfers between devices, to_next_row(): lax.ppermute(block, 'ctx', [(2 * row + side, 2 * after[row] + side) for r...  13.2 us
    pallas_call x1, Pallas kernels, attend(): pl.pallas_call(functools.partial(attend_kernel, slots=len(slots), heads=h...  9.75 us
    ppermute x8, waiting for transfers between devices, to_other_side(): lax.ppermute(block, 'ctx', [(2 * row + side, 2 * row + 1 - side) for row...  9.47 us
    reshape x8, local copies, waits for them, and re-layouts, laid(): return [block.reshape(FT, local_kv) for block in come]  8.87 us
    ppermute x8, starting transfers between devices, to_other_side(): lax.ppermute(block, 'ctx', [(2 * row + side, 2 * row + 1 - side) for row...  8.39 us
    pallas_call x2, Pallas kernels, merged_columns(): pl.pallas_call(merge_kernel, in_specs=[pl.BlockSpec(memory_space=pltpu.SM...  5.85 us
    pallas_call x2, Pallas kernels, vit_attention(): pl.pallas_call(functools.partial(vit_kernel, heads=width // dim, dim=dim)...  5.01 us
    ppermute x6, waiting for transfers between devices, to_next_row(): lax.ppermute(block, 'ctx', [(2 * row + side, 2 * after[row] + side) for r...  4.95 us
  transfers between devices with their start and end apart: 19, of which 10 were waited for; matrix products, arithmetic and copies ran while one was open for 17% of the time, Pallas kernels for 15%

commit v1 on v0

--- a/solution.py
+++ b/solution.py
@@ -21,7 +21,7 @@
 MASKED = -1e30
 VMEM_LIMIT = 16 * 1024 * 1024
 MERGE_VMEM = 52 * 1024 * 1024
-LANGUAGE_VMEM = 58 * 1024 * 1024
+LANGUAGE_VMEM = 54 * 1024 * 1024
 
 
 def contract_last(a, b):
@@ -83,11 +83,11 @@
         return self.blocks
 
 
-def vit_kernel(index_ref, q_ref, k_ref, v_ref, after_ref, *rest, heads, dim):
+def vit_kernel(index_ref, q_ref, k_ref, v_ref, after_ref, *rest, first_row, heads, dim):
     o_ref = rest[0]
     if len(rest) > 1:
         earlier_ref, weight_ref, resid_ref, o_ref, low_ref, high_ref = rest
-    width = q_ref.shape[2]
+    rows, width = o_ref.shape
     to_exp = 1.0 / math.sqrt(dim)
     tiles = {}
     for g in range(heads):
@@ -98,7 +98,9 @@
         inside = (lane >= first) & (lane < last)
         keep = jnp.where(inside, 1.0, 0.0).astype(jnp.bfloat16)
         other = jnp.where(inside, 0.0, 1.0).astype(jnp.bfloat16)
-        scores = contract_last(q_ref[0, :, low:high] * keep, k_ref[0, :, low:high])
+        scores = contract_last(
+            q_ref[0, first_row : first_row + rows, low:high] * keep, k_ref[0, :, low:high]
+        )
         row_max = jnp.max(scores, axis=1, keepdims=True)
         weights = jnp.exp((scores - row_max) * to_exp).astype(jnp.bfloat16)
         mixed = jnp.dot(
@@ -115,9 +117,8 @@
     for at, piece in tiles.items():
         o_ref[:, at : at + piece.shape[1]] = piece.astype(o_ref.dtype)
     if len(rest) > 1:
-        rows = o_ref.shape[0]
-        for part, (context, hidden_ref) in enumerate([(earlier_ref, low_ref), (o_ref, high_ref)]):
-            here = slice(part * rows, (part + 1) * rows)
+        for start, context, hidden_ref in ((0, earlier_ref, low_ref), (first_row, o_ref, high_ref)):
+            here = slice(start, start + hidden_ref.shape[0])
             hidden_ref[...] = resid_ref[here].astype(jnp.float32) + jnp.dot(
                 context[...], weight_ref[...], preferred_element_type=jnp.float32
             )
@@ -125,11 +126,12 @@
 
 def vit_attention(fields, after, part, tp_index, projection=None):
     _, patches, width = fields.shape
-    rows = patches // 2
+    quarter = patches // 4
+    first_row, rows = (0, quarter) if part == 0 else (quarter, patches - quarter)
     dim = VD // VH
     one = pl.BlockSpec((rows, width), lambda f, _: (0, 0))
     in_specs = [
-        pl.BlockSpec((1, rows, width), lambda f, _: (0, part, 0)),
+        pl.BlockSpec((1, patches, width), lambda f, _: (0, 0, 0)),
         pl.BlockSpec((1, patches, width), lambda f, _: (1, 0, 0)),
         pl.BlockSpec((1, patches, width), lambda f, _: (2, 0, 0)),
         pl.BlockSpec(memory_space=pl.ANY),
@@ -138,14 +140,14 @@
     out_shape = [jax.ShapeDtypeStruct((rows, width), jnp.bfloat16)]
     if projection:
         in_specs += [
-            one,
+            pl.BlockSpec((first_row, width), lambda f, _: (0, 0)),
             pl.BlockSpec((width, width), lambda f, index: (index[0], 0)),
             pl.BlockSpec((patches, width), lambda f, _: (0, 0)),
         ]
-        out_specs += [one, one]
-        out_shape += [jax.ShapeDtypeStruct((rows, width), jnp.float32)] * 2
+        out_specs += [pl.BlockSpec((first_row, width), lambda f, _: (0, 0)), one]
+        out_shape += [jax.ShapeDtypeStruct((n, width), jnp.float32) for n in (first_row, rows)]
     return pl.pallas_call(
-        functools.partial(vit_kernel, heads=width // dim, dim=dim),
+        functools.partial(vit_kernel, first_row=first_row, heads=width // dim, dim=dim),
         grid_spec=pltpu.PrefetchScalarGridSpec(
             num_scalar_prefetch=1, grid=(1,), in_specs=in_specs, out_specs=out_specs
         ),

time: 88.6 us -> 86.6 us (0.977)
  the two profiles are of different devices: /device:TPU:22 before, /device:TPU:14 now
where the time goes in v1:
time: 86.6 us; the launch traced here: 84.9 us
  waiting for transfers between devices  25.6 us (30%)
  Pallas kernels  21.7 us (25%)
  starting transfers between devices  17.1 us (20%)
  local copies, waits for them, and re-layouts  12.2 us (14%)
  matrix products  3.69 us (4%)
  other arithmetic  2.32 us (3%)
  between operations  2.31 us (3%)
    ppermute x6, waiting for transfers between devices, to_next_row(): lax.ppermute(block, 'ctx', [(2 * row + side, 2 * after[row] + side) for r...  12.4 us
    pallas_call x1, Pallas kernels, attend(): pl.pallas_call(functools.partial(attend_kernel, slots=len(slots), heads=h...  8.08 us
    ppermute x5, starting transfers between devices, shifted(): lax.ppermute(block, axis, [(i, (i + distance) % count) for i in range(cou...  7.08 us
    reshape x8, local copies, waits for them, and re-layouts, laid(): return [block.reshape(FT, local_kv) for block in come]  6.96 us
    ppermute x8, waiting for transfers between devices, to_other_side(): lax.ppermute(block, 'ctx', [(2 * row + side, 2 * row + 1 - side) for row...  6.87 us
    ppermute x5, waiting for transfers between devices, shifted(): lax.ppermute(block, axis, [(i, (i + distance) % count) for i in range(cou...  6.34 us
    ppermute x8, starting transfers between devices, to_other_side(): lax.ppermute(block, 'ctx', [(2 * row + side, 2 * row + 1 - side) for row...  5.9 us
    pallas_call x2, Pallas kernels, merged_columns(): pl.pallas_call(merge_kernel, in_specs=[pl.BlockSpec(memory_space=pltpu.SM...  5.85 us
  transfers between devices with their start and end apart: 19, of which 10 were waited for; matrix products, arithmetic and copies ran while one was open for 17% of the time, Pallas kernels for 16%

profile of v1, /device:TPU:14, one launch (start us, length us, event | category | flops | bytes accessed | tf_op | source)
XLA Modules:
  0.0 84.9 jit_solution(18375924554476259201)
XLA Ops:
  0.0 1.1 %slice.3.after_ref = bf16[128,4,2,128]{3,2,1,0:T(2,128)(2,1)S(1)} slice(bf16[256,4,2,128]{3,2,1,0:T(2,128)(2,1)} %param.20), slice={[128:256], [0:4], [0:2], [0:128]} | slice | bytes 524288 | tf_op jit(solution)/shard_map/slice | solution.py:472
  1.1 2.7 %collective-permute-start = (bf16[128,4,2,128]{3,2,1,0:T(2,128)(2,1)S(1)}, bf16[128,4,2,128]{3,2,1,0:T(2,128)(2,1)}, u32[]{:S(2)}, u32[]{:S(2)}) collective-permute-start(bf16[128,4,2,128]{3,2,1,0:T(2,128)(2,1)S(1)} %slice.3.after_ref), channel_id=1, source_target_pairs={{0,16},{4,20},{8,24},{12,28},{16,0},{20,4},{24,8},{28,12},{1,17},{... | collective-permute-start | bytes 786440 | tf_op jit(solution)/shard_map/ppermute | solution.py:33
  3.8 1.5 %copy-done = bf16[512,3,640]{2,0,1:T(8,128)(2,1)S(1)} copy-done((bf16[512,3,640]{2,0,1:T(8,128)(2,1)S(1)}, bf16[512,3,640]{2,0,1:T(8,128)(2,1)}, u32[]{:S(2)}) %copy-start) | copy-done | bytes 1966104
  5.3 2.2 %shard_map.109.after_ref.rest_0_ = bf16[128,640]{1,0:T(8,128)(2,1)S(1)} custom-call(s32[1]{0:T(128)} %bitcast.index_ref.block_ref, bf16[3,512,640]{2,1,0:T(8,128)(2,1)S(1)} %bitcast.14, bf16[3,512,640]{2,1,0:T(8,128)(2,1)S(1)} %bitcast.15, bf16[3,512,640]{2,1,0:T(8,128)(2,1)S(1)} %bitcast.16, bf16[128,4,2,128]{3,2,1,0:T(2,128)(2,1)S(1)} %slice.3.after_ref), custom_call_target="tpu_custom_call" | custom-call | flops 1024 | bytes 1024 | tf_op jit(solution)/shard_map/pallas_call | solution.py:149
  8.1 3.4 %shard_map.110 = (bf16[384,640]{1,0:T(8,128)(2,1)}, f32[128,640]{1,0:T(8,128)S(1)}, f32[384,640]{1,0:T(8,128)S(1)}) custom-call(s32[1]{0:T(128)} %bitcast.index_ref.block_ref, bf16[3,512,640]{2,1,0:T(8,128)(2,1)S(1)} %bitcast.17, bf16[3,512,640]{2,1,0:T(8,128)(2,1)S(1)} %bitcast.18, bf16[3,512,640]{2,1,0:T(8,128)(2,1)S(1)} %bitcast.19, ...), custom_call_target="tpu_custom_call" | custom-call | flops 1024 | bytes 1024 | tf_op jit(solution)/shard_map/pallas_call | solution.py:149
  11.5 1.5 %collective-permute-start.4 = (bf16[384,640]{1,0:T(8,128)(2,1)}, bf16[384,640]{1,0:T(8,128)(2,1)}, u32[]{:S(2)}, u32[]{:S(2)}) collective-permute-start(bf16[384,640]{1,0:T(8,128)(2,1)} %get-tuple-element.43), channel_id=1, source_target_pairs={{0,2},{2,0},{1,3},{3,1},{4,6},{6,4},{5,7},{7,5},{8,10},{10,8},{9,1... | collective-permute-start | bytes 1474568 | tf_op jit(solution)/shard_map/ppermute | solution.py:33
  14.4 1.8 %constant_dynamic-slice_fusion = bf16[128,4,2,128]{3,2,1,0:T(2,128)(2,1)} fusion(bf16[256,4,2,128]{3,2,1,0:T(2,128)(2,1)} %param.20, s32[]{:T(128)S(6)} %select_n.20), kind=kLoop, calls=%fused_computation.18 | loop fusion | bytes 524292 | tf_op jit(solution)/shard_map/dynamic_slice | solution.py:491
  17.5 2.0 %convolution_add_fusion.1 = f32[128,640]{1,0:T(8,128)} fusion(f32[128,640]{1,0:T(8,128)S(1)} %get-tuple-element.46, bf16[128,640]{1,0:T(8,128)(2,1)} %collective-permute-done.3, bf16[1280,640]{1,0:T(8,128)(2,1)S(1)} %copy-done.1, s32[]{:T(128)S(6)} %select_n.22), kind=kOutput, calls=%fused_computation.4 | convolution fusion | flops 104939520 | bytes 1638404 | tf_op jit(solution)/shard_map/dot_general | solution.py:499
  19.5 1.0 %broadcast_select_fusion = bf16[128,1,8,128]{3,2,1,0:T(8,128)(2,1)S(1)} fusion(bf16[128,1,8,128]{3,2,1,0:T(8,128)(2,1)} %bitcast.11, bf16[128,1,8,128]{3,2,1,0:T(8,128)(2,1)S(1)} %bitcast.20, pred[]{:T(512)S(6)} %and.8), kind=kLoop, calls=%fused_computation.9 | loop fusion | flops 131072 | bytes 786433 | tf_op jit(solution)/shard_map/jit(_where)/select_n | solution.py:493
  20.6 3.6 %collective-permute-done.4 = bf16[384,640]{1,0:T(8,128)(2,1)} collective-permute-done((bf16[384,640]{1,0:T(8,128)(2,1)}, bf16[384,640]{1,0:T(8,128)(2,1)}, u32[]{:S(2)}, u32[]{:S(2)}) %collective-permute-start.4) | collective-permute-done | bytes 491552 | tf_op jit(solution)/shard_map/ppermute | solution.py:33
  24.2 1.7 %convolution_add_fusion = f32[384,640]{1,0:T(8,128)S(1)} fusion(f32[384,640]{1,0:T(8,128)S(1)} %get-tuple-element.49, bf16[384,640]{1,0:T(8,128)(2,1)} %collective-permute-done.4, bf16[1280,640]{1,0:T(8,128)(2,1)S(1)} %copy-done.1, s32[]{:T(128)S(6)} %select_n.23), kind=kOutput, calls=%fused_computation | convolution fusion | flops 314818560 | bytes 3276804 | tf_op jit(solution)/shard_map/dot_general | solution.py:499
  26.3 1.6 %collective-permute-start.7 = (f32[2,512]{1,0:T(2,128)S(1)}, f32[2,512]{1,0:T(2,128)S(1)}, u32[]{:S(2)}, u32[]{:S(2)}) collective-permute-start(f32[2,512]{1,0:T(2,128)S(1)} %pad_maximum_fusion.1), channel_id=1, source_target_pairs={{0,2},{2,0},{1,3},{3,1},{4,6},{6,4},{5,7},{7,5},{8,10},{10,8},{9,1... | collective-permute-start | bytes 12296 | tf_op jit(solution)/shard_map/ppermute | solution.py:33
  27.8 1.1 %collective-permute-start.6 = (bf16[128,4,2,128]{3,2,1,0:T(2,128)(2,1)S(1)}, bf16[128,4,2,128]{3,2,1,0:T(2,128)(2,1)S(1)}, u32[]{:S(2)}, u32[]{:S(2)}) collective-permute-start(bf16[128,4,2,128]{3,2,1,0:T(2,128)(2,1)S(1)} %collective-permute-done.1), channel_id=1, source_target_pairs={{0,4},{4,0},{8,12},{12,8},{16,20},{20,16},{24,28},{28,24},{1,5},{5... | collective-permute-start | bytes 786440 | tf_op jit(solution)/shard_map/ppermute | solution.py:51
  28.9 1.8 %collective-permute-start.5 = (bf16[128,4,2,128]{3,2,1,0:T(2,128)(2,1)S(1)}, bf16[128,4,2,128]{3,2,1,0:T(2,128)(2,1)S(1)}, u32[]{:S(2)}, u32[]{:S(2)}) collective-permute-start(bf16[128,4,2,128]{3,2,1,0:T(2,128)(2,1)S(1)} %collective-permute-done.1), channel_id=1, source_target_pairs={{0,8},{4,12},{8,24},{12,28},{16,0},{20,4},{24,16},{28,20},{1,9},{5... | collective-permute-start | bytes 786440 | tf_op jit(solution)/shard_map/ppermute | solution.py:43
  31.1 2.9 %shard_map.112 = bf16[128,1024]{1,0:T(8,128)(2,1)S(1)} custom-call(s32[1]{0:T(128)} %bitcast.6.block_ref, bf16[512,640]{1,0:T(8,128)(2,1)S(1)} %add_convert_fusion.x_ref, bf16[4,640,2048]{2,1,0:T(8,128)(2,1)} %w_ref.3), custom_call_target="tpu_custom_call" | custom-call | flops 671088640 | bytes 5898240 | tf_op jit(solution)/shard_map/pallas_call | solution.py:190
  34.8 2.9 %shard_map.111 = f32[128,1024]{1,0:T(8,128)S(1)} custom-call(s32[1]{0:T(128)} %bitcast.index_ref.block_ref, bf16[512,640]{1,0:T(8,128)(2,1)S(1)} %add_convert_fusion.x_ref, bf16[4,640,2048]{2,1,0:T(8,128)(2,1)} %w_ref.3), custom_call_target="tpu_custom_call" | custom-call | flops 671088640 | bytes 5898240 | tf_op jit(solution)/shard_map/pallas_call | solution.py:190
  37.7 2.7 %collective-permute-done.10 = bf16[128,1024]{1,0:T(8,128)(2,1)S(1)} collective-permute-done((bf16[128,1024]{1,0:T(8,128)(2,1)S(1)}, bf16[128,1024]{1,0:T(8,128)(2,1)S(1)}, u32[]{:S(2)}, u32[]{:S(2)}) %collective-permute-start.10) | collective-permute-done | bytes 262176 | tf_op jit(solution)/shard_map/ppermute | solution.py:33
  41.0 2.2 %collective-permute-start.8 = (bf16[128,4,2,128]{3,2,1,0:T(2,128)(2,1)S(1)}, bf16[128,4,2,128]{3,2,1,0:T(2,128)(2,1)S(1)}, u32[]{:S(2)}, u32[]{:S(2)}) collective-permute-start(bf16[128,4,2,128]{3,2,1,0:T(2,128)(2,1)S(1)} %collective-permute-done.5), channel_id=1, source_target_pairs={{0,8},{4,12},{8,24},{12,28},{16,0},{20,4},{24,16},{28,20},{1,9},{5... | collective-permute-start | bytes 786440 | tf_op jit(solution)/shard_map/ppermute | solution.py:43
  43.2 1.5 %collective-permute-start.13 = (bf16[128,1024]{1,0:T(8,128)(2,1)S(1)}, bf16[128,1024]{1,0:T(8,128)(2,1)S(1)}, u32[]{:S(2)}, u32[]{:S(2)}) collective-permute-start(bf16[128,1024]{1,0:T(8,128)(2,1)S(1)} %add_convert_fusion.1.rest_8_), channel_id=1, source_target_pairs={{0,4},{4,0},{8,12},{12,8},{16,20},{20,16},{24,28},{28,24},{1,5},{5... | collective-permute-start | bytes 786440 | tf_op jit(solution)/shard_map/ppermute | solution.py:51
  44.7 2.2 %shard_map.113.place_ref = s32[20]{0:T(128)} custom-call(s32[1]{0:T(128)} %bitcast.7.device_ref, s32[8]{0:T(128)} %vis_pos_ref, s32[8]{0:T(128)} %frame_host_ref.1, s32[16,128]{1,0:T(8,128)} %bitcast.28), custom_call_target="tpu_custom_call" | custom-call | tf_op jit(solution)/shard_map/pallas_call | solution.py:250
  46.9 1.1 %collective-permute-done.11.rest_10_ = bf16[128,1024]{1,0:T(8,128)(2,1)S(1)} collective-permute-done((bf16[128,1024]{1,0:T(8,128)(2,1)S(1)}, bf16[128,1024]{1,0:T(8,128)(2,1)S(1)}, u32[]{:S(2)}, u32[]{:S(2)}) %collective-permute-start.11) | collective-permute-done | bytes 262176 | tf_op jit(solution)/shard_map/ppermute | solution.py:43
  48.3 4.4 %collective-permute-done.8 = bf16[128,4,2,128]{3,2,1,0:T(2,128)(2,1)S(1)} collective-permute-done((bf16[128,4,2,128]{3,2,1,0:T(2,128)(2,1)S(1)}, bf16[128,4,2,128]{3,2,1,0:T(2,128)(2,1)S(1)}, u32[]{:S(2)}, u32[]{:S(2)}) %collective-permute-start.8) | collective-permute-done | bytes 262176 | tf_op jit(solution)/shard_map/ppermute | solution.py:43
  53.0 0.9 %reshape.65.rest_0_ = bf16[128,1024]{1,0:T(8,128)(2,1)} reshape(bf16[128,4,2,128]{3,2,1,0:T(2,128)(2,1)S(1)} %bitcast.23) | data formatting | bytes 524288 | tf_op jit(solution)/shard_map/reshape | solution.py:531
  54.7 0.9 %reshape.67.rest_2_ = bf16[128,1024]{1,0:T(8,128)(2,1)} reshape(bf16[128,4,2,128]{3,2,1,0:T(2,128)(2,1)S(1)} %collective-permute-done.1) | data formatting | bytes 524288 | tf_op jit(solution)/shard_map/reshape | solution.py:531
  56.5 5.2 %collective-permute-done.12.rest_12_ = bf16[128,1024]{1,0:T(8,128)(2,1)S(1)} collective-permute-done((bf16[128,1024]{1,0:T(8,128)(2,1)S(1)}, bf16[128,1024]{1,0:T(8,128)(2,1)S(1)}, u32[]{:S(2)}, u32[]{:S(2)}) %collective-permute-start.12) | collective-permute-done | bytes 262176 | tf_op jit(solution)/shard_map/ppermute | solution.py:43
  62.1 1.6 %collective-permute-start.17 = (bf16[128,1024]{1,0:T(8,128)(2,1)S(1)}, bf16[128,1024]{1,0:T(8,128)(2,1)S(1)}, u32[]{:S(2)}, u32[]{:S(2)}) collective-permute-start(bf16[128,1024]{1,0:T(8,128)(2,1)S(1)} %collective-permute-done.12.rest_12_), channel_id=1, source_target_pairs={{0,4},{4,0},{8,12},{12,8},{16,20},{20,16},{24,28},{28,24},{1,5},{5... | collective-permute-start | bytes 786440 | tf_op jit(solution)/shard_map/ppermute | solution.py:51
  64.5 0.9 %reshape.70.rest_5_ = bf16[128,1024]{1,0:T(8,128)(2,1)} reshape(bf16[128,4,2,128]{3,2,1,0:T(2,128)(2,1)S(1)} %collective-permute-done.9) | data formatting | bytes 524288 | tf_op jit(solution)/shard_map/reshape | solution.py:531
  66.3 1.7 %collective-permute-done.14.rest_14_ = bf16[128,1024]{1,0:T(8,128)(2,1)S(1)} collective-permute-done((bf16[128,1024]{1,0:T(8,128)(2,1)S(1)}, bf16[128,1024]{1,0:T(8,128)(2,1)S(1)}, u32[]{:S(2)}, u32[]{:S(2)}) %collective-permute-start.14) | collective-permute-done | bytes 262176 | tf_op jit(solution)/shard_map/ppermute | solution.py:43
  68.5 1.8 %collective-permute-done.16 = bf16[128,4,2,128]{3,2,1,0:T(2,128)(2,1)S(1)} collective-permute-done((bf16[128,4,2,128]{3,2,1,0:T(2,128)(2,1)S(1)}, bf16[128,4,2,128]{3,2,1,0:T(2,128)(2,1)S(1)}, u32[]{:S(2)}, u32[]{:S(2)}) %collective-permute-start.16) | collective-permute-done | bytes 262176 | tf_op jit(solution)/shard_map/ppermute | solution.py:51
  71.1 1.9 %collective-permute-done.17.rest_13_ = bf16[128,1024]{1,0:T(8,128)(2,1)S(1)} collective-permute-done((bf16[128,1024]{1,0:T(8,128)(2,1)S(1)}, bf16[128,1024]{1,0:T(8,128)(2,1)S(1)}, u32[]{:S(2)}, u32[]{:S(2)}) %collective-permute-start.17) | collective-permute-done | bytes 262176 | tf_op jit(solution)/shard_map/ppermute | solution.py:51
  73.1 2.8 %collective-permute-done.18.rest_15_ = bf16[128,1024]{1,0:T(8,128)(2,1)S(1)} collective-permute-done((bf16[128,1024]{1,0:T(8,128)(2,1)S(1)}, bf16[128,1024]{1,0:T(8,128)(2,1)S(1)}, u32[]{:S(2)}, u32[]{:S(2)}) %collective-permute-start.18) | collective-permute-done | bytes 262176 | tf_op jit(solution)/shard_map/ppermute | solution.py:51
  76.6 8.1 %shard_map.114 = bf16[256,2048]{1,0:T(8,128)(2,1)} custom-call(s32[20]{0:T(128)} %shard_map.113.place_ref, bf16[256,2048]{1,0:T(8,128)(2,1)} %q_ref.1, bf16[128,1024]{1,0:T(8,128)(2,1)} %reshape.65.rest_0_, bf16[128,1024]{1,0:T(8,128)(2,1)} %reshape.66.rest_1_, bf16[128,1024]{1,0:T(8,128)(2,1)} %reshape.67.rest_2_, bf16[128,1024]{1,0:T(8,128)(2,1)} %reshape.68.rest_3_, ...), custom_call_target="tpu_custom_call" | custom-call | flops 6442450944 | bytes 6291456 | tf_op jit(solution)/shard_map/pallas_call | solution.py:415
  (65 shorter events, 10.0 us)
Async XLA Ops:
  1.1 18.3 %collective-permute-start = (bf16[128,4,2,128]{3,2,1,0:T(2,128)(2,1)S(1)}, bf16[128,4,2,128]{3,2,1,0:T(2,128)(2,1)}, u32[]{:S(2)}, u32[]{:S(2)}) collective-permute-start(bf16[128,4,2,128]{3,2,1,0:T(2,128)(2,1)S(1)} %slice.3.after_ref), channel_id=1, source_target_pairs={{0,16},{4,20},{8,24},{12,28},{16,0},{20,4},{24,8},{28,12},{1,17},{... | collective-permute-start | bytes 786440 | tf_op jit(solution)/shard_map/ppermute | solution.py:33
  5.3 2.8 %copy-start.1 = (bf16[1280,640]{1,0:T(8,128)(2,1)S(1)}, bf16[1280,640]{1,0:T(8,128)(2,1)}, u32[]{:S(2)}) copy-start(bf16[1280,640]{1,0:T(8,128)(2,1)} %rest_1_.1) | copy-start | bytes 4915204
  5.3 2.8 %copy-start.2 = (bf16[512,640]{1,0:T(8,128)(2,1)S(1)}, bf16[512,640]{1,0:T(8,128)(2,1)}, u32[]{:S(2)}) copy-start(bf16[512,640]{1,0:T(8,128)(2,1)} %rest_2_.1) | copy-start | bytes 1966084
  7.5 5.5 %copy-start.8 = (s32[8]{0:T(128)S(1)}, s32[8]{0:T(128)}, u32[]{:S(2)}) copy-start(s32[8]{0:T(128)} %vis_pos_ref) | copy-start | bytes 100
  7.5 9.9 %collective-permute-start.3 = (bf16[128,640]{1,0:T(8,128)(2,1)S(1)}, bf16[128,640]{1,0:T(8,128)(2,1)}, u32[]{:S(2)}, u32[]{:S(2)}) collective-permute-start(bf16[128,640]{1,0:T(8,128)(2,1)S(1)} %shard_map.109.after_ref.rest_0_), channel_id=1, source_target_pairs={{0,2},{2,0},{1,3},{3,1},{4,6},{6,4},{5,7},{7,5},{8,10},{10,8},{9,1... | collective-permute-start | bytes 491528 | tf_op jit(solution)/shard_map/ppermute | solution.py:33
  11.5 12.7 %collective-permute-start.4 = (bf16[384,640]{1,0:T(8,128)(2,1)}, bf16[384,640]{1,0:T(8,128)(2,1)}, u32[]{:S(2)}, u32[]{:S(2)}) collective-permute-start(bf16[384,640]{1,0:T(8,128)(2,1)} %get-tuple-element.43), channel_id=1, source_target_pairs={{0,2},{2,0},{1,3},{3,1},{4,6},{6,4},{5,7},{7,5},{8,10},{10,8},{9,1... | collective-permute-start | bytes 1474568 | tf_op jit(solution)/shard_map/ppermute | solution.py:33
  17.5 2.0 %copy-start.4 = (bf16[128,4,2,128]{3,2,1,0:T(2,128)(2,1)S(1)}, bf16[128,4,2,128]{3,2,1,0:T(2,128)(2,1)}, u32[]{:S(2)}) copy-start(bf16[128,4,2,128]{3,2,1,0:T(2,128)(2,1)} %constant_dynamic-slice_fusion) | copy-start | bytes 786436
  20.5 7.4 %collective-permute-start.2 = (bf16[128,4,2,128]{3,2,1,0:T(2,128)(2,1)S(1)}, bf16[128,4,2,128]{3,2,1,0:T(2,128)(2,1)S(1)}, u32[]{:S(2)}, u32[]{:S(2)}) collective-permute-start(bf16[128,4,2,128]{3,2,1,0:T(2,128)(2,1)S(1)} %bitcast.21), channel_id=1, source_target_pairs={{0,4},{4,0},{8,12},{12,8},{16,20},{20,16},{24,28},{28,24},{1,5},{5... | collective-permute-start | bytes 786440 | tf_op jit(solution)/shard_map/ppermute | solution.py:51
  20.5 7.3 %collective-permute-start.1 = (bf16[128,4,2,128]{3,2,1,0:T(2,128)(2,1)S(1)}, bf16[128,4,2,128]{3,2,1,0:T(2,128)(2,1)S(1)}, u32[]{:S(2)}, u32[]{:S(2)}) collective-permute-start(bf16[128,4,2,128]{3,2,1,0:T(2,128)(2,1)S(1)} %bitcast.22), channel_id=1, source_target_pairs={{0,8},{4,12},{8,24},{12,28},{16,0},{20,4},{24,16},{28,20},{1,9},{5... | collective-permute-start | bytes 786440 | tf_op jit(solution)/shard_map/ppermute | solution.py:43
  25.9 4.8 %copy-start.6 = (f32[640]{0:T(1024)S(1)}, f32[640]{0:T(1024)}, u32[]{:S(2)}) copy-start(f32[640]{0:T(1024)} %param.15) | copy-start | bytes 7684
  26.0 4.8 %copy-start.7 = (f32[640]{0:T(1024)S(1)}, f32[640]{0:T(1024)}, u32[]{:S(2)}) copy-start(f32[640]{0:T(1024)} %param.14) | copy-start | bytes 7684
  26.3 4.5 %collective-permute-start.7 = (f32[2,512]{1,0:T(2,128)S(1)}, f32[2,512]{1,0:T(2,128)S(1)}, u32[]{:S(2)}, u32[]{:S(2)}) collective-permute-start(f32[2,512]{1,0:T(2,128)S(1)} %pad_maximum_fusion.1), channel_id=1, source_target_pairs={{0,2},{2,0},{1,3},{3,1},{4,6},{6,4},{5,7},{7,5},{8,10},{10,8},{9,1... | collective-permute-start | bytes 12296 | tf_op jit(solution)/shard_map/ppermute | solution.py:33
  27.8 9.9 %collective-permute-start.6 = (bf16[128,4,2,128]{3,2,1,0:T(2,128)(2,1)S(1)}, bf16[128,4,2,128]{3,2,1,0:T(2,128)(2,1)S(1)}, u32[]{:S(2)}, u32[]{:S(2)}) collective-permute-start(bf16[128,4,2,128]{3,2,1,0:T(2,128)(2,1)S(1)} %collective-permute-done.1), channel_id=1, source_target_pairs={{0,4},{4,0},{8,12},{12,8},{16,20},{20,16},{24,28},{28,24},{1,5},{5... | collective-permute-start | bytes 786440 | tf_op jit(solution)/shard_map/ppermute | solution.py:51
  28.9 8.8 %collective-permute-start.5 = (bf16[128,4,2,128]{3,2,1,0:T(2,128)(2,1)S(1)}, bf16[128,4,2,128]{3,2,1,0:T(2,128)(2,1)S(1)}, u32[]{:S(2)}, u32[]{:S(2)}) collective-permute-start(bf16[128,4,2,128]{3,2,1,0:T(2,128)(2,1)S(1)} %collective-permute-done.1), channel_id=1, source_target_pairs={{0,8},{4,12},{8,24},{12,28},{16,0},{20,4},{24,16},{28,20},{1,9},{5... | collective-permute-start | bytes 786440 | tf_op jit(solution)/shard_map/ppermute | solution.py:43
  34.0 6.4 %collective-permute-start.10 = (bf16[128,1024]{1,0:T(8,128)(2,1)S(1)}, bf16[128,1024]{1,0:T(8,128)(2,1)S(1)}, u32[]{:S(2)}, u32[]{:S(2)}) collective-permute-start(bf16[128,1024]{1,0:T(8,128)(2,1)S(1)} %shard_map.112), channel_id=1, source_target_pairs={{0,2},{2,0},{1,3},{3,1},{4,6},{6,4},{5,7},{7,5},{8,10},{10,8},{9,1... | collective-permute-start | bytes 786440 | tf_op jit(solution)/shard_map/ppermute | solution.py:33
  40.5 24.1 %copy-start.5 = (bf16[128,1024]{1,0:T(8,128)(2,1)}, bf16[128,1024]{1,0:T(8,128)(2,1)S(1)}, u32[]{:S(2)}) copy-start(bf16[128,1024]{1,0:T(8,128)(2,1)S(1)} %add_convert_fusion.1.rest_8_) | copy-start | bytes 786436
  40.5 7.5 %collective-permute-start.11 = (bf16[128,1024]{1,0:T(8,128)(2,1)S(1)}, bf16[128,1024]{1,0:T(8,128)(2,1)S(1)}, u32[]{:S(2)}, u32[]{:S(2)}) collective-permute-start(bf16[128,1024]{1,0:T(8,128)(2,1)S(1)} %add_convert_fusion.1.rest_8_), channel_id=1, source_target_pairs={{0,8},{4,12},{8,24},{12,28},{16,0},{20,4},{24,16},{28,20},{1,9},{5... | collective-permute-start | bytes 786440 | tf_op jit(solution)/shard_map/ppermute | solution.py:43
  40.6 7.7 %collective-permute-start.9 = (bf16[128,4,2,128]{3,2,1,0:T(2,128)(2,1)S(1)}, bf16[128,4,2,128]{3,2,1,0:T(2,128)(2,1)S(1)}, u32[]{:S(2)}, u32[]{:S(2)}) collective-permute-start(bf16[128,4,2,128]{3,2,1,0:T(2,128)(2,1)S(1)} %collective-permute-done.5), channel_id=1, source_target_pairs={{0,4},{4,0},{8,12},{12,8},{16,20},{20,16},{24,28},{28,24},{1,5},{5... | collective-permute-start | bytes 786440 | tf_op jit(solution)/shard_map/ppermute | solution.py:51
  41.0 11.7 %collective-permute-start.8 = (bf16[128,4,2,128]{3,2,1,0:T(2,128)(2,1)S(1)}, bf16[128,4,2,128]{3,2,1,0:T(2,128)(2,1)S(1)}, u32[]{:S(2)}, u32[]{:S(2)}) collective-permute-start(bf16[128,4,2,128]{3,2,1,0:T(2,128)(2,1)S(1)} %collective-permute-done.5), channel_id=1, source_target_pairs={{0,8},{4,12},{8,24},{12,28},{16,0},{20,4},{24,16},{28,20},{1,9},{5... | collective-permute-start | bytes 786440 | tf_op jit(solution)/shard_map/ppermute | solution.py:43
  43.2 13.3 %collective-permute-start.13 = (bf16[128,1024]{1,0:T(8,128)(2,1)S(1)}, bf16[128,1024]{1,0:T(8,128)(2,1)S(1)}, u32[]{:S(2)}, u32[]{:S(2)}) collective-permute-start(bf16[128,1024]{1,0:T(8,128)(2,1)S(1)} %add_convert_fusion.1.rest_8_), channel_id=1, source_target_pairs={{0,4},{4,0},{8,12},{12,8},{16,20},{20,16},{24,28},{28,24},{1,5},{5... | collective-permute-start | bytes 786440 | tf_op jit(solution)/shard_map/ppermute | solution.py:51
  48.0 16.6 %copy-start.9 = (bf16[128,1024]{1,0:T(8,128)(2,1)}, bf16[128,1024]{1,0:T(8,128)(2,1)S(1)}, u32[]{:S(2)}) copy-start(bf16[128,1024]{1,0:T(8,128)(2,1)S(1)} %collective-permute-done.11.rest_10_) | copy-start | bytes 786436
  52.6 9.0 %collective-permute-start.12 = (bf16[128,1024]{1,0:T(8,128)(2,1)S(1)}, bf16[128,1024]{1,0:T(8,128)(2,1)S(1)}, u32[]{:S(2)}, u32[]{:S(2)}) collective-permute-start(bf16[128,1024]{1,0:T(8,128)(2,1)S(1)} %collective-permute-done.11.rest_10_), channel_id=1, source_target_pairs={{0,8},{4,12},{8,24},{12,28},{16,0},{20,4},{24,16},{28,20},{1,9},{5... | collective-permute-start | bytes 786440 | tf_op jit(solution)/shard_map/ppermute | solution.py:43
  52.6 13.7 %collective-permute-start.15 = (bf16[128,1024]{1,0:T(8,128)(2,1)S(1)}, bf16[128,1024]{1,0:T(8,128)(2,1)S(1)}, u32[]{:S(2)}, u32[]{:S(2)}) collective-permute-start(bf16[128,1024]{1,0:T(8,128)(2,1)S(1)} %collective-permute-done.11.rest_10_), channel_id=1, source_target_pairs={{0,4},{4,0},{8,12},{12,8},{16,20},{20,16},{24,28},{28,24},{1,5},{5... | collective-permute-start | bytes 786440 | tf_op jit(solution)/shard_map/ppermute | solution.py:51
  56.5 19.4 %copy-start.10 = (bf16[128,1024]{1,0:T(8,128)(2,1)}, bf16[128,1024]{1,0:T(8,128)(2,1)S(1)}, u32[]{:S(2)}) copy-start(bf16[128,1024]{1,0:T(8,128)(2,1)S(1)} %collective-permute-done.13.rest_9_) | copy-start | bytes 786436
  61.6 14.2 %copy-start.11 = (bf16[128,1024]{1,0:T(8,128)(2,1)}, bf16[128,1024]{1,0:T(8,128)(2,1)S(1)}, u32[]{:S(2)}) copy-start(bf16[128,1024]{1,0:T(8,128)(2,1)S(1)} %collective-permute-done.12.rest_12_) | copy-start | bytes 786436
  61.6 6.4 %collective-permute-start.14 = (bf16[128,1024]{1,0:T(8,128)(2,1)S(1)}, bf16[128,1024]{1,0:T(8,128)(2,1)S(1)}, u32[]{:S(2)}, u32[]{:S(2)}) collective-permute-start(bf16[128,1024]{1,0:T(8,128)(2,1)S(1)} %collective-permute-done.12.rest_12_), channel_id=1, source_target_pairs={{0,8},{4,12},{8,24},{12,28},{16,0},{20,4},{24,16},{28,20},{1,9},{5... | collective-permute-start | bytes 786440 | tf_op jit(solution)/shard_map/ppermute | solution.py:43
  61.6 8.6 %collective-permute-start.16 = (bf16[128,4,2,128]{3,2,1,0:T(2,128)(2,1)S(1)}, bf16[128,4,2,128]{3,2,1,0:T(2,128)(2,1)S(1)}, u32[]{:S(2)}, u32[]{:S(2)}) collective-permute-start(bf16[128,4,2,128]{3,2,1,0:T(2,128)(2,1)S(1)} %collective-permute-done.8), channel_id=1, source_target_pairs={{0,4},{4,0},{8,12},{12,8},{16,20},{20,16},{24,28},{28,24},{1,5},{5... | collective-permute-start | bytes 786440 | tf_op jit(solution)/shard_map/ppermute | solution.py:51
  62.1 11.0 %collective-permute-start.17 = (bf16[128,1024]{1,0:T(8,128)(2,1)S(1)}, bf16[128,1024]{1,0:T(8,128)(2,1)S(1)}, u32[]{:S(2)}, u32[]{:S(2)}) collective-permute-start(bf16[128,1024]{1,0:T(8,128)(2,1)S(1)} %collective-permute-done.12.rest_12_), channel_id=1, source_target_pairs={{0,4},{4,0},{8,12},{12,8},{16,20},{20,16},{24,28},{28,24},{1,5},{5... | collective-permute-start | bytes 786440 | tf_op jit(solution)/shard_map/ppermute | solution.py:51
  66.3 9.6 %copy-start.12 = (bf16[128,1024]{1,0:T(8,128)(2,1)}, bf16[128,1024]{1,0:T(8,128)(2,1)S(1)}, u32[]{:S(2)}) copy-start(bf16[128,1024]{1,0:T(8,128)(2,1)S(1)} %collective-permute-done.15.rest_11_) | copy-start | bytes 786436
  68.0 7.9 %copy-start.13 = (bf16[128,1024]{1,0:T(8,128)(2,1)}, bf16[128,1024]{1,0:T(8,128)(2,1)S(1)}, u32[]{:S(2)}) copy-start(bf16[128,1024]{1,0:T(8,128)(2,1)S(1)} %collective-permute-done.14.rest_14_) | copy-start | bytes 786436
  68.0 7.9 %collective-permute-start.18 = (bf16[128,1024]{1,0:T(8,128)(2,1)S(1)}, bf16[128,1024]{1,0:T(8,128)(2,1)S(1)}, u32[]{:S(2)}, u32[]{:S(2)}) collective-permute-start(bf16[128,1024]{1,0:T(8,128)(2,1)S(1)} %collective-permute-done.14.rest_14_), channel_id=1, source_target_pairs={{0,4},{4,0},{8,12},{12,8},{16,20},{20,16},{24,28},{28,24},{1,5},{5... | collective-permute-start | bytes 786440 | tf_op jit(solution)/shard_map/ppermute | solution.py:51
  73.1 2.8 %copy-start.14 = (bf16[128,1024]{1,0:T(8,128)(2,1)}, bf16[128,1024]{1,0:T(8,128)(2,1)S(1)}, u32[]{:S(2)}) copy-start(bf16[128,1024]{1,0:T(8,128)(2,1)S(1)} %collective-permute-done.17.rest_13_) | copy-start | bytes 786436
  (3 other events, 3.9 us)
